TPU v7x, 128 devices: a whole 4x4x4 slice. The times are simulated.
128 devices in a mesh: dp: 16 (over z, x), tensor: 8 (over y, core).
Axes of the slice: x: 4, y: 4, z: 4, core: 2. Of those that a mesh axis runs over, the one named last changes fastest.
Arguments:
- queries: bfloat16 [1024, 32, 128], P('dp'), may hold values from -5 to 5
- new_keys: bfloat16 [1024, 2, 128], P('dp'), may hold values from -5 to 5
- new_values: bfloat16 [1024, 2, 128], P('dp'), may hold values from -5 to 5
- key_cache: bfloat16 [1024, 2, 256, 128], P('dp', None, 'tensor'), may hold values from -160 to 160
- value_cache: bfloat16 [1024, 2, 256, 128], P('dp', None, 'tensor'), may hold values from -5 to 5
- lengths: int32 [1024], P('dp'), may hold values from 2 to 256, as said below
- residual_in: bfloat16 [1024, 4096], P(('dp', 'tensor')), may hold values from -24 to 24
- query_gain: float32 [128], replicated, may hold values from 0.1 to 1.9
- key_gain: float32 [128], replicated, may hold values from 0.1 to 1.9
- out_proj: bfloat16 [4096, 4096], P('tensor'), may hold values from -0.09375 to 0.09375
- norm_gain: float32 [4096], replicated, may hold values from 0.1 to 1.9
- expert_ids: int32 [1024, 8], P(('dp', 'tensor')), may hold values from 0 to 127, all different within a row; in each aligned block of 8 rows (0 to 7, 8 to 15, ...) at most 3 rows name the same one
- gate_weights: float32 [1024, 8], P(('dp', 'tensor')), may hold values from 0.05 to 1
- expert_gate: bfloat16 [128, 4096, 768], P(('dp', 'tensor')), may hold values from -0.09375 to 0.09375
- expert_up: bfloat16 [128, 4096, 768], P(('dp', 'tensor')), may hold values from -0.09375 to 0.09375
- expert_down: bfloat16 [128, 768, 4096], P(('dp', 'tensor')), may hold values from -0.21875 to 0.21875
Outputs:
- mixed: bfloat16 [1024, 4096], P(('dp', 'tensor'))
Inputs may be any that keep to these rules, and one draw needn't show every extreme that they name: `expert_ids`: rows are taken in aligned blocks of 8; within a block no expert is named by more than 3 rows, a bound that some block reaches. `lengths`: each group of 64 rows has a row with 256 positions in use.
All inputs are finite; a program needn't handle non-finite values.
Results may differ from a plain program's by a relative error of at most 0.013.
Values may be sent and summed in bfloat16 or wider, within the bound.
A program may use at most 128 MiB of HBM per device.

v0:
```python
import jax
import jax.numpy as jnp
from jax import lax
from jax.sharding import PartitionSpec as P

CAP = 3


def rms_scale(values, gain):
    mean_sq = jnp.mean(values * values, axis=-1, keepdims=True)
    return values * lax.rsqrt(mean_sq + 1e-06) * gain


def expert_rows(block, expert_gate, expert_up, expert_down):
    width = block.shape[-1]
    flat_rows = block.reshape(-1, width)
    gate_val = jnp.dot(flat_rows, expert_gate[0], preferred_element_type=jnp.float32)
    up_val = jnp.dot(flat_rows, expert_up[0], preferred_element_type=jnp.float32)
    activation = (jax.nn.silu(gate_val) * up_val).astype(jnp.bfloat16)
    result = jnp.dot(activation, expert_down[0], preferred_element_type=jnp.float32).astype(
        jnp.bfloat16
    )
    return result.reshape(block.shape)


def shards(
    queries,
    new_keys,
    new_values,
    key_cache,
    value_cache,
    lengths,
    residual_in,
    query_gain,
    key_gain,
    out_proj,
    norm_gain,
    expert_ids,
    gate_weights,
    expert_gate,
    expert_up,
    expert_down,
):
    tensor_pos = lax.axis_index("tensor")
    tensor_count = lax.axis_size("tensor")
    dp_count = lax.axis_size("dp")
    row_total, head_total, head_dim = queries.shape
    kv_total = key_cache.shape[1]
    cache_local = key_cache.shape[2]
    group_size = head_total // kv_total
    query_norm = rms_scale(queries.astype(jnp.float32), query_gain).astype(jnp.bfloat16)
    key_norm = rms_scale(new_keys.astype(jnp.float32), key_gain).astype(jnp.bfloat16)
    grouped = query_norm.reshape(row_total, kv_total, group_size, head_dim)
    scaling = head_dim ** (-0.5)
    cache_scores = (
        jnp.einsum("rgqd,rgpd->rgqp", grouped, key_cache, preferred_element_type=jnp.float32)
        * scaling
    )
    new_score = (
        jnp.einsum("rgqd,rgd->rgq", grouped, key_norm, preferred_element_type=jnp.float32) * scaling
    )
    positions = tensor_pos * cache_local + jnp.arange(cache_local, dtype=jnp.int32)
    included = (positions[None, :] < lengths[:, None])[:, None, None, :]
    local_top = jnp.maximum(jnp.max(jnp.where(included, cache_scores, -1e30), axis=-1), new_score)
    score_top = lax.pmax(local_top, "tensor")
    cache_weights = jnp.where(included, jnp.exp(cache_scores - score_top[..., None]), 0.0).astype(
        jnp.bfloat16
    )
    new_weight = jnp.exp(new_score - score_top).astype(jnp.bfloat16)
    own_new = (tensor_pos == 0).astype(jnp.float32) * new_weight.astype(jnp.float32)
    numerator = jnp.einsum(
        "rgqp,rgpd->rgqd", cache_weights, value_cache, preferred_element_type=jnp.float32
    )
    numerator = numerator + own_new[..., None] * new_values.astype(jnp.float32)[:, :, None, :]
    weight_sum = jnp.sum(cache_weights.astype(jnp.float32), axis=-1) + own_new
    numer_own, denom_own = (
        lax.psum_scatter(
            numerator.reshape(row_total, head_total * head_dim).astype(jnp.bfloat16),
            "tensor",
            scatter_dimension=1,
            tiled=True,
        ).astype(jnp.float32),
        lax.psum_scatter(
            weight_sum.reshape(row_total, head_total).astype(jnp.bfloat16),
            "tensor",
            scatter_dimension=1,
            tiled=True,
        ).astype(jnp.float32),
    )
    heads_own = denom_own.shape[1]
    attn_own = (
        (numer_own.reshape(row_total, heads_own, head_dim) / denom_own[..., None])
        .reshape(row_total, heads_own * head_dim)
        .astype(jnp.bfloat16)
    )
    share_rows = residual_in.shape[0]
    partial_sum = jnp.dot(attn_own, out_proj, preferred_element_type=jnp.float32)
    whole_sum = lax.psum(partial_sum.astype(jnp.bfloat16), "tensor").astype(jnp.float32)
    proj_rows = lax.dynamic_slice_in_dim(whole_sum, tensor_pos * share_rows, share_rows, 0)
    hidden = residual_in.astype(jnp.float32) + proj_rows
    normed = rms_scale(hidden, norm_gain).astype(jnp.bfloat16)
    expert_total = expert_gate.shape[0] * dp_count * tensor_count
    capacity = CAP
    top_count = expert_ids.shape[1]
    flat_ids = expert_ids.reshape(-1)
    onehot = (flat_ids[:, None] == jnp.arange(expert_total, dtype=jnp.int32)[None, :]).astype(
        jnp.int32
    )
    earlier = jnp.cumsum(onehot, axis=0) - onehot
    slot_index = jnp.sum(earlier * onehot, axis=1)
    target = flat_ids * capacity + slot_index
    slot_ids = jnp.arange(expert_total * capacity, dtype=jnp.int32)
    placed = target[:, None] == slot_ids[None, :]
    dispatch_map = jnp.sum(
        placed.reshape(share_rows, top_count, -1).astype(jnp.int32), axis=1
    ).astype(jnp.bfloat16)
    outgoing = jnp.einsum(
        "ts,td->sd", dispatch_map, normed, preferred_element_type=jnp.float32
    ).astype(jnp.bfloat16)
    outgoing = outgoing.reshape(expert_total, capacity, -1)
    route_weights = (gate_weights / jnp.sum(gate_weights, axis=1, keepdims=True)).astype(
        jnp.bfloat16
    )
    combine_map = jnp.sum(
        jnp.where(placed, route_weights.reshape(-1)[:, None], jnp.zeros((), jnp.bfloat16)).reshape(
            share_rows, top_count, -1
        ),
        axis=1,
    )
    computed = expert_rows(
        lax.all_to_all(outgoing, ("dp", "tensor"), split_axis=0, concat_axis=0, tiled=True),
        expert_gate,
        expert_up,
        expert_down,
    )
    returned = lax.all_to_all(computed, ("dp", "tensor"), split_axis=0, concat_axis=0, tiled=True)
    moe_sum = jnp.dot(
        combine_map,
        returned.reshape(expert_total * capacity, -1),
        preferred_element_type=jnp.float32,
    )
    return (hidden + moe_sum).astype(jnp.bfloat16)


def solution(mesh):
    return jax.shard_map(
        shards,
        mesh=mesh,
        in_specs=(
            P("dp", None, None),
            P("dp", None, None),
            P("dp", None, None),
            P("dp", None, "tensor", None),
            P("dp", None, "tensor", None),
            P("dp"),
            P(("dp", "tensor"), None),
            P(),
            P(),
            P("tensor", None),
            P(),
            P(("dp", "tensor"), None),
            P(("dp", "tensor"), None),
            P(("dp", "tensor"), None, None),
            P(("dp", "tensor"), None, None),
            P(("dp", "tensor"), None, None),
        ),
        out_specs=P(("dp", "tensor"), None),
        check_vma=False,
    )
```

profile of v0, /device:TPU:1, one launch (start us, length us, event | category | flops | bytes accessed | tf_op | source)
XLA Modules:
  0.0 320.1 jit_solution(12639388721475537391)
XLA Ops:
  6.6 1.5 fusion.17
  8.1 0.7 broadcast_compare_fusion
  8.8 1.4 fusion.19
  10.2 2.0 select_reduce_fusion
  12.3 0.1 fusion.25
  12.5 0.1 fusion.35
  12.6 0.4 fusion.29
  13.1 23.8 %pmax.7 = f32[64,2,16]{0,2,1:T(8,128)S(1)} all-reduce(f32[64,2,16]{0,2,1:T(8,128)S(1)} %fusion.37), channel_id=1, replica_groups=mesh['dp'=16,'tensor'=8] {'tensor'}, use_global_device_ids=true, to_apply=%region_3.4 | all-reduce | flops 2048 | bytes 16384 | tf_op jit(solution)/shard_map/pmax | solution.py:65
  37.0 0.8 convert_reduce_fusion
  38.0 0.8 fusion.16
  38.8 1.0 copy.47
  39.9 0.6 dynamic-slice
  41.2 15.5 %all-reduce = bf16[64,32]{0,1:T(8,128)(2,1)S(1)} all-reduce(bf16[64,32]{0,1:T(8,128)(2,1)S(1)} %bitcast.56), channel_id=3, replica_groups=mesh['dp'=16,'tensor'=8] {'tensor'}, use_global_device_ids=true, to_apply=%region_6.7.clone | all-reduce | flops 2048 | bytes 8192
  57.1 0.2 select_reduce_fusion.1
  57.4 13.5 %reduce-scatter.2.cloned.1.call-done = bf16[64,512]{1,0:T(8,128)(2,1)} async-done(((bf16[64,4096]{1,0:T(8,128)(2,1)}), bf16[64,512]{1,0:T(8,128)(2,1)}) %reduce-scatter.2.cloned.1.call-update) | async-done | bytes 65552 | tf_op jit(solution)/shard_map/reduce_scatter | solution.py:77
  70.8 0.1 div.42
  71.0 3.9 %convolution_convert_fusion.1 = bf16[64,4096]{1,0:T(8,128)(2,1)} fusion(bf16[512,4096]{1,0:T(8,128)(2,1)} %param.25, f32[8,8,4,128]{3,2,1,0:T(4,128)S(1)} %bitcast.54, bf16[64,512]{1,0:T(8,128)(2,1)} %reduce-scatter.2.cloned.1.call-done), kind=kOutput, calls=%fused_computation.8 | convolution fusion | flops 268795904 | bytes 4915200 | tf_op jit(solution)/shard_map/dot_general | solution.py:97
  75.0 60.2 %all-reduce.3.cloned.1.call-done = bf16[64,4096]{1,0:T(8,128)(2,1)} async-done(((bf16[64,4096]{1,0:T(8,128)(2,1)}), bf16[64,4096]{1,0:T(8,128)(2,1)}) %all-reduce.3.cloned.1.call-update) | async-done | bytes 524304 | tf_op jit(solution)/shard_map/psum | solution.py:98
  135.2 1.0 multiply_reduce_fusion
  136.2 3.6 %convolution_convert_fusion = bf16[384,4096]{1,0:T(8,128)(2,1)} fusion(bf16[8,4096]{1,0:T(8,128)(2,1)S(1)} %copy-done.1, f32[4096]{0:T(1024)S(1)} %copy-done.4, f32[8]{0:T(128)S(1)} %add_rsqrt_fusion.2, bf16[64,4096]{1,0:T(8,128)(2,1)} %all-reduce.3.cloned.1.call-done, s32[]{:T(128)S(6)} %select_n.17, s32[8,384]{1,0:T(8,128)S(1)} %convert_reduce_fusion.1), kind=kOutput, calls=%fused_computation.7 | convolution fusion | flops 26938368 | bytes 3305508 | tf_op jit(solution)/shard_map/ts,td->sd/dot_general | solution.py:117
  139.8 7.1 %reshape.116 = bf16[128,3,4096]{2,1,0:T(4,128)(2,1)} reshape(bf16[384,4096]{1,0:T(8,128)(2,1)} %convolution_convert_fusion) | data formatting | bytes 6291456 | tf_op jit(solution)/shard_map/reshape | solution.py:120
  146.9 62.7 %all_to_all.10 = bf16[128,3,4096]{2,1,0:T(4,128)(2,1)} all-to-all(bf16[128,3,4096]{2,1,0:T(4,128)(2,1)} %reshape.116), channel_id=1, replica_groups=mesh['dp'=16,'tensor'=8] {'dp','tensor'}, dimensions={0} | all-to-all | bytes 6291456 | tf_op jit(solution)/shard_map/all_to_all | solution.py:131
  209.6 7.4 %reshape.117 = bf16[384,4096]{1,0:T(8,128)(2,1)} reshape(bf16[128,3,4096]{2,1,0:T(4,128)(2,1)} %all_to_all.10) | data formatting | bytes 6291456 | tf_op jit(solution)/shard_map/reshape | solution.py:16
  217.0 6.3 %fusion.4 = f32[384,768]{1,0:T(8,128)S(1)} fusion(bf16[384,4096]{1,0:T(8,128)(2,1)} %reshape.117, bf16[1,4096,768]{2,1,0:T(8,128)(2,1)} %param.29), kind=kOutput, calls=%fused_computation.4 | convolution fusion | flops 2415919104 | bytes 10616832 | tf_op jit(solution)/shard_map/dot_general | solution.py:17
  223.3 13.9 %fusion.6 = bf16[384,4096]{1,0:T(8,128)(2,1)} fusion(bf16[1,768,4096]{2,1,0:T(8,128)(2,1)} %param.31, bf16[384,4096]{1,0:T(8,128)(2,1)} %reshape.117, bf16[1,4096,768]{2,1,0:T(8,128)(2,1)} %param.30, f32[384,768]{1,0:T(8,128)S(1)} %fusion.4), kind=kOutput, calls=%fused_computation.6 | convolution fusion | flops 4835180544 | bytes 20054016 | tf_op jit(solution)/shard_map/dot_general | solution.py:20
  237.3 7.1 %reshape.118 = bf16[128,3,4096]{2,1,0:T(4,128)(2,1)} reshape(bf16[384,4096]{1,0:T(8,128)(2,1)} %fusion.6) | data formatting | bytes 6291456 | tf_op jit(solution)/shard_map/reshape | solution.py:23
  244.4 5.5 %all-to-all-start.1 = ((bf16[128,3,4096]{2,1,0:T(4,128)(2,1)}), bf16[128,3,4096]{2,1,0:T(4,128)(2,1)}, u32[]{:S(2)}, u32[]{:S(2)}) async-start(bf16[128,3,4096]{2,1,0:T(4,128)(2,1)} %reshape.118), calls=%async_computation.2 | async-start | bytes 8388608 | tf_op jit(solution)/shard_map/all_to_all | solution.py:136
  249.9 0.1 reduce_sum.82
  250.1 0.1 fusion.34
  250.2 52.6 %all-to-all-done.1 = bf16[128,3,4096]{2,1,0:T(4,128)(2,1)} async-done(((bf16[128,3,4096]{2,1,0:T(4,128)(2,1)}), bf16[128,3,4096]{2,1,0:T(4,128)(2,1)}, u32[]{:S(2)}, u32[]{:S(2)}) %all-to-all-start.1) | async-done | bytes 3145760 | tf_op jit(solution)/shard_map/all_to_all | solution.py:136
  302.8 7.4 %reshape.119 = bf16[384,4096]{1,0:T(8,128)(2,1)} reshape(bf16[128,3,4096]{2,1,0:T(4,128)(2,1)} %all-to-all-done.1) | data formatting | bytes 6291456 | tf_op jit(solution)/shard_map/reshape | solution.py:139
  310.2 3.0 fusion.9
  (43 shorter events, 1.2 us)
Async XLA Ops:
  6.5 31.5 %copy-start = (bf16[64,2,32,128]{3,2,1,0:T(8,128)(2,1)S(1)}, bf16[64,2,32,128]{3,2,1,0:T(8,128)(2,1)}, u32[]{:S(2)}) copy-start(bf16[64,2,32,128]{3,2,1,0:T(8,128)(2,1)} %param.20) | copy-start | bytes 3145732
  6.5 5.8 %copy-start.2 = (bf16[64,2,128]{2,1,0:T(2,128)(2,1)S(1)}, bf16[64,2,128]{2,1,0:T(2,128)(2,1)}, u32[]{:S(2)}) copy-start(bf16[64,2,128]{2,1,0:T(2,128)(2,1)} %param.17) | copy-start | bytes 98308
  6.5 5.9 %copy-start.7 = (f32[128]{0:T(128)S(1)}, f32[128]{0:T(128)}, u32[]{:S(2)}) copy-start(f32[128]{0:T(128)} %param.24) | copy-start | bytes 1540
  6.5 64.3 %reduce-scatter.2.cloned.1.call-start = ((), (), s32[]{:S(2)}) async-start(), calls=%async_computation.3 | async-start | bytes 589824 | tf_op jit(solution)/shard_map/reduce_scatter | solution.py:77
  8.8 29.2 %copy-start.3 = (bf16[64,2,128]{2,1,0:T(2,128)(2,1)S(1)}, bf16[64,2,128]{2,1,0:T(2,128)(2,1)}, u32[]{:S(2)}) copy-start(bf16[64,2,128]{2,1,0:T(2,128)(2,1)} %param.18) | copy-start | bytes 98308
  38.0 1.9 copy-start.8
  38.0 18.8 %copy-start.5 = (s32[8,8]{1,0:T(8,128)S(1)}, s32[8,8]{1,0:T(8,128)}, u32[]{:S(2)}) copy-start(s32[8,8]{1,0:T(8,128)} %param.27) | copy-start | bytes 772
  39.8 95.4 %copy-start.1 = (bf16[8,4096]{1,0:T(8,128)(2,1)S(1)}, bf16[8,4096]{1,0:T(8,128)(2,1)}, u32[]{:S(2)}) copy-start(bf16[8,4096]{1,0:T(8,128)(2,1)} %param.22) | copy-start | bytes 196612
  39.8 96.4 %copy-start.4 = (f32[4096]{0:T(1024)S(1)}, f32[4096]{0:T(1024)}, u32[]{:S(2)}) copy-start(f32[4096]{0:T(1024)} %param.26) | copy-start | bytes 49156
  39.9 95.3 %all-reduce.3.cloned.1.call-start = ((), (), s32[]{:S(2)}) async-start(), calls=%async_computation.4 | async-start | bytes 1048576 | tf_op jit(solution)/shard_map/psum | solution.py:98
  244.4 5.5 %copy-start.6 = (f32[8,8]{1,0:T(8,128)S(1)}, f32[8,8]{1,0:T(8,128)}, u32[]{:S(2)}) copy-start(f32[8,8]{1,0:T(8,128)} %param.28) | copy-start | bytes 772
  244.4 58.5 %all-to-all-start.1 = ((bf16[128,3,4096]{2,1,0:T(4,128)(2,1)}), bf16[128,3,4096]{2,1,0:T(4,128)(2,1)}, u32[]{:S(2)}, u32[]{:S(2)}) async-start(bf16[128,3,4096]{2,1,0:T(4,128)(2,1)} %reshape.118), calls=%async_computation.2 | async-start | bytes 8388608 | tf_op jit(solution)/shard_map/all_to_all | solution.py:136
Sparse Core Ops, SparseCore 0:
  40.0 30.8 reduce-scatter.1
  75.0 60.1 all-reduce.2
where the time goes:
time: 321 us; the launch traced here: 320 us
  waiting for transfers between devices  126 us (39%)
  blocking collectives  102 us (32%)
  matrix products  33.9 us (11%)
  local copies, waits for them, and re-layouts  31.4 us (10%)
  between operations  14.3 us (4%)
  other arithmetic  6.5 us (2%)
  starting transfers between devices  5.56 us (2%)
    all_to_all x1, blocking collectives, shards(): lax.all_to_all(outgoing, ('dp', 'tensor'), split_axis=0, concat_axis=0, t...  62.7 us
    psum x1, waiting for transfers between devices, shards(): lax.psum(partial_sum.astype(jnp.bfloat16), 'tensor').astype(jnp.float32)  60.2 us
    all_to_all x1, waiting for transfers between devices, shards(): lax.all_to_all(computed, ('dp', 'tensor'), split_axis=0, concat_axis=0, t...  52.6 us
    pmax x1, blocking collectives, shards(): score_top = lax.pmax(local_top, 'tensor')  23.8 us
    unnamed x1, blocking collectives  15.5 us
    dot_general x1, matrix products, expert_rows(): jnp.dot(activation, expert_down[0], preferred_element_type=jnp.float32)  13.9 us
    reduce_scatter x1, waiting for transfers between devices, shards(): lax.psum_scatter(numerator.reshape(row_total, head_total * head_dim).asty...  13.5 us
    reshape x1, local copies, waits for them, and re-layouts, shards(): returned.reshape(expert_total * capacity, -1)  7.42 us
  transfers between devices with their start and end apart: 3, of which 3 were waited for; matrix products, arithmetic and copies ran while one was open for 1% of the time, Pallas kernels for 0%

commit v1 on v0

v1 whole, which is shorter than its diff:
```python
import jax
import jax.numpy as jnp
from jax import lax
from jax.experimental import pallas as pl
from jax.experimental.pallas import tpu as pltpu
from jax.sharding import PartitionSpec as P

MESH = pl.DeviceIdType.MESH
F32 = jnp.float32
BF16 = jnp.bfloat16
VMEM = pltpu.VMEM

D = 4096
HALF = 2048
FFW = 768
SLOTS = 96
EPS = 1e-6
LOW = -1e30
OFFSET = (0, 640, 1280)
WIDTH = (640, 640, 768)
ORDER = (("x", "y", "z"), ("y", "z", "x"), ("z", "x", "y"))
PARTS = (0, 1, 2)


def iota(shape, dim):
    return lax.broadcasted_iota(jnp.int32, shape, dim)


def dot(a, b):
    return jnp.dot(a, b, preferred_element_type=F32)


def kernel(
    q_ref, nk_ref, nv_ref, kc_ref, vc_ref, len_ref, res_ref, qg_ref, kg_ref, ng_ref, ids_ref, gw_ref,
    wp_hbm, wg_hbm, wu_hbm, wd_hbm,
    out_ref,
    wp, wg, wu, wd,
    num_f, num_b, stat, stat_t, coef, rec_num, rec_stat, attn,
    send_b, rec_b, hidden, sq_own, sq_rec,
    meta, plane_meta,
    g0, g1, g2, disp, comb,
    xs0, xs1, xs2, xr0, xr1, xr2, x_full, perm, perm_t, act, act_p,
    ys0, ys1, ys2, yr0, yr1, yr2,
    ps0, ps1, ps2, rb0, rb1, rb2, ra_s0, ra_s1, ra_s2, ra_r0, ra_r1, ra_r2,
    fin_s, fin_r,
    w_sem, loc_sem, send_sem, recv_sem,
):
    g, xs, xr, ys, yr = (g0, g1, g2), (xs0, xs1, xs2), (xr0, xr1, xr2), (ys0, ys1, ys2), (yr0, yr1, yr2)
    ps, rb, ra_s, ra_r = (ps0, ps1, ps2), (rb0, rb1, rb2), (ra_s0, ra_s1, ra_s2), (ra_r0, ra_r1, ra_r2)
    dp = lax.axis_index("dp")
    t = lax.axis_index("tensor")
    here = {"z": dp // 4, "x": dp % 4, "y": t // 2, "c": t % 2}
    c = here["c"]

    def device(**moved):
        at = dict(here, **moved)
        return (at["z"] * 4 + at["x"], at["y"] * 2 + at["c"])

    def along(axis, k):
        return (here[axis] + k) % 4

    def tensor_peer(k):
        return (dp, (t + k) % 8)

    counter = [0]
    sent = []

    def remote(src, dst, to):
        i = counter[0]
        counter[0] += 1
        copy = pltpu.make_async_remote_copy(
            src_ref=src,
            dst_ref=dst,
            send_sem=send_sem.at[i],
            recv_sem=recv_sem.at[i],
            device_id=to,
            device_id_type=MESH,
        )
        copy.start()
        sent.append(copy)
        return copy

    sibling = device(c=1 - c)

    weights = []
    for i, (src, dst) in enumerate(
        ((wp_hbm, wp), (wg_hbm.at[0], wg), (wu_hbm.at[0], wu), (wd_hbm.at[0], wd))
    ):
        weights.append(pltpu.make_async_copy(src, dst, w_sem.at[i]))
        weights[-1].start()

    barrier = pltpu.get_barrier_semaphore()
    peers = [tensor_peer(k) for k in range(1, 8)]
    for axis in ("x", "z"):
        for k in (1, 2, 3):
            for core in (0, 1):
                peers.append(device(**{axis: along(axis, k), "c": core}))
    for peer in peers:
        pl.semaphore_signal(barrier, inc=1, device_id=peer, device_id_type=MESH)
    pl.semaphore_wait(barrier, len(peers))

    own_rows = pl.ds(pl.multiple_of(c * 8, 8), 8)
    other_rows = pl.ds(pl.multiple_of((1 - c) * 8, 8), 8)
    own_cols = pl.ds(pl.multiple_of(c * HALF, HALF), HALF)
    other_cols = pl.ds(pl.multiple_of((1 - c) * HALF, HALF), HALF)
    hidden[own_rows, :] = res_ref[:, own_cols].astype(F32)
    fin_s[0] = res_ref[:, other_cols].astype(F32)
    res_copy = remote(fin_s.at[0], hidden.at[own_rows, :], sibling)

    gw = gw_ref[...]
    route = (gw / jnp.sum(gw, axis=1, keepdims=True)).astype(BF16)
    put = iota((8, 128), 1) - iota((8, 128), 0)
    ids = ids_ref[...].astype(F32).astype(BF16)
    table = dot(ids, (put == 0).astype(F32).astype(BF16)) + dot(
        route, (put == 8).astype(F32).astype(BF16)
    )
    z, x, y = here["z"], here["x"], here["y"]
    meta[z, x, y, c] = table
    spread = [
        remote(meta.at[z, x, y, c], meta.at[z, x, y, c], tensor_peer(k)) for k in range(1, 8)
    ]

    scaling = 128.0**-0.5
    first = (t == 0).astype(F32)
    shuffle = (iota((128, 128), 1) == (iota((128, 128), 0) % 8) * 16 + iota((128, 128), 0) // 8)
    shuffle = shuffle.astype(F32).astype(BF16)
    lane_row = iota((1, 256), 1) // 32
    lane_pos = iota((1, 256), 1) % 32 + t * 32
    own_block = (iota((128, 256), 0) % 8) == (iota((128, 256), 1) // 32)
    ones = jnp.ones((256, 128), BF16)
    lane = iota((8, 128), 1)
    stat[...] = jnp.zeros_like(stat)

    def attend(blk, carry):
        at = pl.multiple_of(blk * 8, 8)
        rows = pl.ds(at, 8)
        limit = jnp.zeros((1, 256), jnp.int32)
        for r in range(8):
            limit = jnp.where(lane_row == r, len_ref[at + r], limit)
        bias = jnp.where(lane_pos < limit, 0.0, LOW)
        stats = jnp.zeros((8, 128), F32)
        for kv in range(2):
            q = q_ref[rows, pl.ds(kv * 16, 16), :].astype(F32).reshape(128, 128)
            q = q * lax.rsqrt(jnp.mean(q * q, axis=1, keepdims=True) + EPS) * qg_ref[...]
            q = dot(shuffle, q.astype(BF16)).astype(BF16)
            nk = nk_ref[rows, kv, :].astype(F32)
            nk = nk * lax.rsqrt(jnp.mean(nk * nk, axis=1, keepdims=True) + EPS) * kg_ref[...]
            nk = nk.astype(BF16).astype(F32)
            nv = nv_ref[rows, kv, :].astype(F32)
            keys = kc_ref[rows, kv].reshape(256, 128)
            values = vc_ref[rows, kv].reshape(256, 128)
            score = lax.dot_general(
                q, keys, (((1,), (1,)), ((), ())), preferred_element_type=F32
            )
            score = jnp.where(own_block, score * scaling + bias, LOW)
            fresh = (q.astype(F32).reshape(16, 8, 128) * nk[None]).reshape(128, 128)
            fresh = jnp.sum(fresh, axis=1, keepdims=True) * scaling
            top = jnp.maximum(jnp.max(score, axis=1, keepdims=True), fresh)
            weight = jnp.exp(score - top).astype(BF16)
            new_weight = jnp.exp(fresh - top).astype(BF16).astype(F32) * first
            number = dot(weight, values)
            total = dot(weight, ones) + new_weight
            number = number.reshape(16, 8, 128) + new_weight.reshape(16, 8, 1) * nv[None]
            top = jnp.broadcast_to(top, (128, 128)).reshape(16, 8, 128)
            total = total.reshape(16, 8, 128)
            for i in range(16):
                head = kv * 16 + i
                num_f[head, rows, :] = number[i]
                column = 8 * (head // 4) + head % 4
                stats = jnp.where(lane == column, top[i], stats)
                stats = jnp.where(lane == column + 4, total[i], stats)
        stat[rows, :] = stats
        return carry

    lax.fori_loop(0, 8, attend, 0)
    stat_t[...] = stat[...].T
    num_b[...] = num_f[...].astype(BF16)
    partials = []
    for k in (4, 3, 5, 2, 6, 1, 7):
        to = (t + k) % 8
        tile = pl.ds(pl.multiple_of(to * 8, 8), 8)
        partials.append(remote(stat_t.at[tile, :], rec_stat.at[k], (dp, to)))
        partials.append(remote(num_b.at[pl.ds(to * 4, 4)], rec_num.at[k], (dp, to)))

    for copy in spread:
        copy.wait_recv()
    spread = [
        remote(meta.at[z, x], meta.at[z, x], device(x=along("x", k))) for k in (1, 2, 3)
    ]
    rec_num[0] = num_b[pl.ds(t * 4, 4)]
    rec_stat[0] = stat_t[pl.ds(pl.multiple_of(t * 8, 8), 8), :]
    row = iota((384, 384), 0)
    col = iota((384, 384), 1)
    zz, yy, xx, rest = row // 96, (row // 24) % 4, (row // 6) % 4, row % 6
    perm[0] = (col == xx * 96 + zz * 24 + yy * 6 + rest).astype(F32).astype(BF16)
    perm[1] = (col == yy * 96 + xx * 24 + zz * 6 + rest).astype(F32).astype(BF16)
    zz, yy, xx, rest = col // 96, (col // 24) % 4, (col // 6) % 4, col % 6
    perm_t[0] = (row == xx * 96 + zz * 24 + yy * 6 + rest).astype(F32).astype(BF16)
    perm_t[1] = (row == yy * 96 + xx * 24 + zz * 6 + rest).astype(F32).astype(BF16)

    for copy in partials:
        copy.wait_recv()
    tops = [rec_stat[k][0:4] for k in range(8)]
    best = tops[0]
    for top in tops[1:]:
        best = jnp.maximum(best, top)
    scale = [jnp.exp(top - best) for top in tops]
    whole = scale[0] * rec_stat[0][4:8]
    for k in range(1, 8):
        whole = whole + scale[k] * rec_stat[k][4:8]
    coef[...] = jnp.zeros_like(coef)
    for k in range(8):
        coef[8 * k : 8 * k + 4, :] = scale[k] / whole
    columns = coef[...].T
    for j in range(4):
        out = jnp.zeros((64, 128), F32)
        for k in range(8):
            out = out + columns[0:64, 8 * k + j : 8 * k + j + 1] * rec_num[k, j].astype(F32)
        attn[:, 128 * j : 128 * j + 128] = out.astype(BF16)

    for copy in spread:
        copy.wait_recv()
    spread = [remote(meta.at[z], meta.at[z], device(z=along("z", k))) for k in (1, 2, 3)]

    weights[0].wait()
    for half in (0, 1):
        for tile in range(0, HALF, 512):
            send_b[half, :, tile : tile + 512] = dot(
                attn[...], wp[:, half * HALF + tile : half * HALF + tile + 512]
            ).astype(BF16)
    shares = []
    for k in (4, 3, 5, 2, 6, 1, 7):
        to = (t + k) % 8
        rows = pl.ds(pl.multiple_of((to // 2) * 16, 16), 16)
        shares.append(remote(send_b.at[to % 2, rows, :], rec_b.at[k], (dp, to)))

    for copy in spread:
        copy.wait_recv()
    before = iota((256, 256), 0)
    after = iota((256, 256), 1)
    earlier = ((before // 8 == after // 8) & (before < after)).astype(F32).astype(BF16)
    slot_base = ((iota((1, 256), 1) // 8) * 3).astype(F32)
    slot_id = iota((SLOTS, 256), 0).astype(F32)
    for p in PARTS:
        a, b, last = ORDER[p]
        for ib in range(4):
            for ia in range(4):
                at = dict(here, **{a: ia, b: ib})
                plane_meta[pl.ds((ib * 4 + ia) * 16, 16), :] = meta[
                    at["z"], at["x"], at["y"]
                ].reshape(16, 128)
        table = plane_meta[...].T
        chosen, gates = table[0:8], table[8:16]
        for k in range(4):
            for core in range(2):
                at = dict(here, **{last: k, "c": core})
                expert = (at["z"] * 32 + at["x"] * 8 + at["y"] * 2 + at["c"]).astype(F32)
                hit = (chosen == expert).astype(F32)
                used = jnp.sum(hit, axis=0, keepdims=True)
                gate = jnp.sum(hit * gates, axis=0, keepdims=True)
                rank = dot(jnp.broadcast_to(used, (8, 256)).astype(BF16), earlier)[0:1]
                slot = jnp.where(used > 0.5, slot_base + rank, -1.0)
                match = slot == slot_id
                first_slot = (k * 2 + core) * SLOTS
                disp[p, first_slot : first_slot + SLOTS, :] = match.astype(F32).astype(BF16)
                comb[p, first_slot : first_slot + SLOTS, :] = jnp.where(match, gate, 0.0).astype(BF16)

    res_copy.wait_recv()
    for copy in shares:
        copy.wait_recv()
    rows = pl.ds(pl.multiple_of(y * 16, 16), 16)
    total = send_b[c, rows, :].astype(F32)
    for k in range(1, 8):
        total = total + rec_b[k].astype(F32)
    value = hidden[...] + total
    hidden[...] = value
    squares = jnp.sum(value * value, axis=1, keepdims=True)
    sq_own[...] = jnp.broadcast_to(squares, (16, 128))
    sq_copy = remote(sq_own, sq_rec, sibling)
    sq_copy.wait_recv()
    mean = (squares + sq_rec[:, 0:1]) * (1.0 / D)
    normed = (value * lax.rsqrt(mean + EPS) * ng_ref[pl.ds(c, 1), :]).astype(BF16)

    stage = []
    for p in PARTS:
        a, b, last = ORDER[p]
        g[p][here[b], here[a]] = normed[:, OFFSET[p] : OFFSET[p] + WIDTH[p]]
        unit = g[p].at[here[b], here[a]]
        stage.append([remote(unit, unit, device(**{a: along(a, k)})) for k in (2, 1, 3)])
    for p in PARTS:
        a, b, last = ORDER[p]
        for copy in stage[p]:
            copy.wait_recv()
        unit = g[p].at[here[b]]
        stage[p] = [remote(unit, unit, device(**{b: along(b, k)})) for k in (2, 1, 3)]
    arriving, locals_in = [], []
    for p in PARTS:
        a, b, last = ORDER[p]
        for copy in stage[p]:
            copy.wait_recv()
        plane = g[p][...].reshape(256, WIDTH[p])
        copies = []
        for k in (2, 1, 3, 0):
            to = along(last, k)
            wanted = disp[p, pl.ds(pl.multiple_of(to * 2 * SLOTS, 2 * SLOTS), 2 * SLOTS), :]
            xs[p][k] = dot(wanted, plane).astype(BF16).reshape(2, SLOTS, WIDTH[p])
            for j in (0, 1):
                core = (c + j) % 2
                src = xs[p].at[k, core]
                dst = xr[p].at[c, here[last]]
                if k == 0 and j == 0:
                    local = pltpu.make_async_copy(src, dst, loc_sem.at[p])
                    local.start()
                    locals_in.append(local)
                else:
                    copies.append(remote(src, dst, device(**{last: to, "c": core})))
        arriving.append(copies)
    for p in PARTS:
        for copy in arriving[p]:
            copy.wait_recv()
        locals_in[p].wait()
        for half in (0, 1):
            cols = slice(half * HALF + OFFSET[p], half * HALF + OFFSET[p] + WIDTH[p])
            block = xr[p][half].reshape(384, WIDTH[p])
            if p > 0:
                block = dot(perm[p - 1], block).astype(BF16)
            x_full[:, cols] = block

    for copy in weights[1:]:
        copy.wait()

    def expert(n, carry):
        cols = pl.ds(pl.multiple_of(n * 256, 256), 256)
        gate = dot(x_full[...], wg[:, cols])
        up = dot(x_full[...], wu[:, cols])
        act[:, cols] = (gate / (1.0 + jnp.exp(-gate)) * up).astype(BF16)
        return carry

    lax.fori_loop(0, FFW // 256, expert, 0)

    arriving, locals_out = [], []
    for p in PARTS:
        a, b, last = ORDER[p]
        if p == 0:
            act_p[...] = act[...]
        else:
            act_p[...] = dot(perm_t[p - 1], act[...]).astype(BF16)
        for half in (0, 1):
            cols = slice(half * HALF + OFFSET[p], half * HALF + OFFSET[p] + WIDTH[p])
            ys[p][half] = dot(act_p[...], wd[:, cols]).astype(BF16).reshape(4, SLOTS, WIDTH[p])
        copies = []
        for k in (2, 1, 3, 0):
            to = along(last, k)
            for j in (0, 1):
                core = (c + j) % 2
                src = ys[p].at[core, to]
                dst = yr[p].at[here[last] * 2 + c]
                if k == 0 and j == 0:
                    local = pltpu.make_async_copy(src, dst, loc_sem.at[3 + p])
                    local.start()
                    locals_out.append(local)
                else:
                    copies.append(remote(src, dst, device(**{last: to, "c": core})))
        arriving.append(copies)
    stage = []
    for p in PARTS:
        a, b, last = ORDER[p]
        for copy in arriving[p]:
            copy.wait_recv()
        locals_out[p].wait()
        summed = lax.dot_general(
            comb[p], yr[p][...].reshape(8 * SLOTS, WIDTH[p]), (((0,), (0,)), ((), ())),
            preferred_element_type=F32,
        )
        ps[p][...] = summed.astype(BF16).reshape(4, 64, WIDTH[p])
        copies = []
        for k in (2, 1, 3):
            to = along(b, k)
            copies.append(remote(ps[p].at[to], rb[p].at[k], device(**{b: to})))
        stage.append(copies)
    for p in PARTS:
        a, b, last = ORDER[p]
        for copy in stage[p]:
            copy.wait_recv()
        total = ps[p][here[b]].astype(F32)
        for k in (1, 2, 3):
            total = total + rb[p][k].astype(F32)
        ra_s[p][...] = total.astype(BF16).reshape(4, 16, WIDTH[p])
        copies = []
        for k in (2, 1, 3):
            to = along(a, k)
            copies.append(remote(ra_s[p].at[to], ra_r[p].at[k], device(**{a: to})))
        stage[p] = copies
    for p in PARTS:
        a, b, last = ORDER[p]
        for copy in stage[p]:
            copy.wait_recv()
        total = ra_s[p][here[a]].astype(F32)
        for k in (1, 2, 3):
            total = total + ra_r[p][k].astype(F32)
        cols = slice(OFFSET[p], OFFSET[p] + WIDTH[p])
        hidden[:, cols] = hidden[:, cols] + total

    fin_s[1] = hidden[other_rows, :]
    fin = remote(fin_s.at[1], fin_r, sibling)
    out_ref[:, own_cols] = hidden[own_rows, :].astype(BF16)
    fin.wait_recv()
    out_ref[:, other_cols] = fin_r[...].astype(BF16)
    for copy in sent:
        copy.wait_send()


COPIES = 7 + 3 + 3 + 1 + 14 + 7 + 1 + 9 + 9 + 21 + 21 + 9 + 9 + 1


def shards(
    queries, new_keys, new_values, key_cache, value_cache, lengths, residual_in, query_gain, key_gain,
    out_proj, norm_gain, expert_ids, gate_weights, expert_gate, expert_up, expert_down,
):
    vmem = pl.BlockSpec(memory_space=pltpu.VMEM)
    anywhere = pl.BlockSpec(memory_space=pl.ANY)

    def each(shape_of, dtype=BF16):
        return [VMEM(shape_of(w), dtype) for w in WIDTH]

    return pl.pallas_call(
        kernel,
        out_shape=jax.ShapeDtypeStruct((8, D), BF16),
        in_specs=[vmem] * 5 + [pl.BlockSpec(memory_space=pltpu.SMEM)] + [vmem] * 6 + [anywhere] * 4,
        out_specs=vmem,
        scratch_shapes=[
            VMEM((512, D), BF16), VMEM((D, FFW), BF16), VMEM((D, FFW), BF16), VMEM((FFW, D), BF16),
            VMEM((32, 64, 128), F32), VMEM((32, 64, 128), BF16), VMEM((128, 128), F32),
            VMEM((128, 128), F32), VMEM((128, 128), F32), VMEM((8, 4, 64, 128), BF16),
            VMEM((8, 8, 128), F32), VMEM((64, 512), BF16),
            VMEM((2, 64, HALF), BF16), VMEM((8, 16, HALF), BF16), VMEM((16, HALF), F32),
            VMEM((16, 128), F32), VMEM((16, 128), F32),
            VMEM((4, 4, 4, 2, 8, 128), F32), VMEM((256, 128), F32),
            *each(lambda w: (4, 4, 16, w)),
            VMEM((3, 8 * SLOTS, 256), BF16), VMEM((3, 8 * SLOTS, 256), BF16),
            *each(lambda w: (4, 2, SLOTS, w)),
            *each(lambda w: (2, 4, SLOTS, w)),
            VMEM((384, D), BF16), VMEM((2, 384, 384), BF16), VMEM((2, 384, 384), BF16),
            VMEM((384, FFW), BF16), VMEM((384, FFW), BF16),
            *each(lambda w: (2, 4, SLOTS, w)),
            *each(lambda w: (8, SLOTS, w)),
            *each(lambda w: (4, 64, w)), *each(lambda w: (4, 64, w)),
            *each(lambda w: (4, 16, w)), *each(lambda w: (4, 16, w)),
            VMEM((2, 8, HALF), F32), VMEM((8, HALF), F32),
            pltpu.SemaphoreType.DMA((4,)), pltpu.SemaphoreType.DMA((6,)),
            pltpu.SemaphoreType.DMA((COPIES,)), pltpu.SemaphoreType.DMA((COPIES,)),
        ],
        compiler_params=pltpu.CompilerParams(
            collective_id=0, has_side_effects=True, vmem_limit_bytes=60 * 2**20
        ),
        cost_estimate=pl.CostEstimate(flops=10**10, bytes_accessed=26 * 2**20, transcendentals=10**6),
    )(
        queries, new_keys, new_values, key_cache, value_cache, lengths, residual_in,
        query_gain.reshape(1, 128), key_gain.reshape(1, 128), norm_gain.reshape(2, HALF),
        expert_ids, gate_weights, out_proj, expert_gate, expert_up, expert_down,
    )


def solution(mesh):
    rows = P(("dp", "tensor"), None)
    experts = P(("dp", "tensor"), None, None)
    cache = P("dp", None, "tensor", None)
    heads = P("dp", None, None)
    return jax.shard_map(
        shards,
        mesh=mesh,
        in_specs=(
            heads, heads, heads, cache, cache, P("dp"), rows, P(), P(),
            P("tensor", None), P(), rows, rows, experts, experts, experts,
        ),
        out_specs=rows,
        check_vma=False,
    )
```

time: 321 us -> 107 us (0.33)
  waiting for transfers between devices: 126 us -> 0 us
  Pallas kernels: 0 us -> 104 us
  blocking collectives: 102 us -> 0 us
  matrix products: 33.9 us -> 0 us
  local copies, waits for them, and re-layouts: 31.4 us -> 2.81 us
  between operations: 14.3 us -> 0.01 us
  other arithmetic: 6.5 us -> 0 us
  starting transfers between devices: 5.56 us -> 0 us
    pallas_call x0 -> x1, Pallas kernels: none -> 104 us  [shards(): pl.pallas_call(kernel, out_shape=jax.ShapeDtypeStruct((8, D), BF16), in_s...]
    all_to_all x1 -> x0, blocking collectives: 62.7 us -> none  [shards(): lax.all_to_all(outgoing, ('dp', 'tensor'), split_axis=0, concat_axis=0, t...]
    psum x1 -> x0, waiting for transfers between devices: 60.2 us -> none  [shards(): lax.psum(partial_sum.astype(jnp.bfloat16), 'tensor').astype(jnp.float32)]
    all_to_all x1 -> x0, waiting for transfers between devices: 52.6 us -> none  [shards(): lax.all_to_all(computed, ('dp', 'tensor'), split_axis=0, concat_axis=0, t...]
    dot_general x8 -> x0, matrix products: 33.9 us -> none  [the longest x1 13.9 us: expert_rows(): jnp.dot(activation, expert_down[0], preferred_element_type=jnp.float32)]
    reshape x4 -> x1, local copies, waits for them, and re-layouts: 29 us -> 1.33 us  [shards(): norm_gain.reshape(2, HALF)]
    pmax x1 -> x0, blocking collectives: 23.8 us -> none  [shards(): score_top = lax.pmax(local_top, 'tensor')]
    unnamed x1 -> x0, blocking collectives: 15.5 us -> none
  transfers between devices with their start and end apart: 3 -> 0, of which waited for: 3 -> 0; matrix products, arithmetic and copies ran while one was open for 1% -> 0% of each run, Pallas kernels for 0% -> 0%
where the time goes in v1:
time: 107 us
  Pallas kernels  104 us (97%)
  local copies, waits for them, and re-layouts  2.81 us (3%)
    pallas_call x1, Pallas kernels, shards(): pl.pallas_call(kernel, out_shape=jax.ShapeDtypeStruct((8, D), BF16), in_s...  104 us

profile of v1, /device:TPU:1, one launch (start us, length us, event | category | flops | bytes accessed | tf_op | source)
XLA Modules:
  0.0 106.7 jit_solution(2680220347694606860)
XLA Ops:
  0.0 1.3 %reshape.11.ng_ref = f32[2,2048]{1,0:T(2,128)} reshape(f32[4096]{0:T(1024)} %param.26) | data formatting | bytes 32768 | tf_op jit(solution)/shard_map/reshape | solution.py:459
  1.3 103.8 %shard_map.154 = bf16[8,4096]{1,0:T(8,128)(2,1)} custom-call(bf16[64,32,128]{2,1,0:T(8,128)(2,1)} %q_ref.1, bf16[64,2,128]{2,1,0:T(2,128)(2,1)} %nk_ref.1, bf16[64,2,128]{2,1,0:T(2,128)(2,1)} %nv_ref.1, bf16[64,2,32,128]{3,2,1,0:T(8,128)(2,1)} %kc_ref.1, bf16[64,2,32,128]{3,2,1,0:T(8,128)(2,1)} %vc_ref.1, s32[64]{0:T(128)} %len_ref.1, ...), custom_call_target="tpu_custom_call" | custom-call | flops 10000000000 | bytes 27262976 | tf_op jit(solution)/shard_map/pallas_call | solution.py:426
  105.2 1.5 %copy.18 = bf16[8,4096]{1,0:T(8,128)(2,1)} copy(bf16[8,4096]{1,0:T(8,128)(2,1)} %shard_map.154) | data formatting | bytes 131072

commit v2 on v1

v2 whole, which is shorter than its diff:
```python
import jax
import jax.numpy as jnp
from jax import lax
from jax.experimental import pallas as pl
from jax.experimental.pallas import tpu as pltpu
from jax.sharding import PartitionSpec as P

MESH = pl.DeviceIdType.MESH
F32 = jnp.float32
BF16 = jnp.bfloat16
VMEM = pltpu.VMEM

D = 4096
HALF = 2048
FFW = 768
SLOTS = 96
EPS = 1e-6
LOW = -1e30
ORDER = (("x", "y", "z"), ("y", "z", "x"), ("z", "x", "y"))
WAVES = (((2, 0, 384), (0, 384, 256), (1, 640, 384)), ((2, 1024, 384), (0, 1408, 384), (1, 1792, 256)))
PARTS = tuple(part for wave in WAVES for part in wave)
FORTH = ((0, 1, 2), (3, 4, 5))
BACK = ((3, 4, 5), (0, 1, 2))


def iota(shape, dim):
    return lax.broadcasted_iota(jnp.int32, shape, dim)


def dot(a, b):
    return jnp.dot(a, b, preferred_element_type=F32)


def kernel(
    q_ref, nk_ref, nv_ref, kc_ref, vc_ref, len_ref, res_ref, qg_ref, kg_ref, ng_ref, ids_ref, gw_ref,
    wp_hbm, wg_hbm, wu_hbm, wd_hbm,
    out_ref,
    wp, wg, wu, wd,
    num_f, num_b, stat, stat_t, coef, rec_num, rec_stat, attn,
    pair_s, pair_r, send_b, rec_b, hidden, sq_own, sq_rec,
    table_s, table_r, packed, meta, plane_meta, disp, comb,
    x_full, perm, perm_t, acc, act, act_p,
    g, xs, xr, ys, yr, ps, rb, ra_s, ra_r,
    fin_s, fin_r,
    w_sem, loc_sem, send_sem, recv_sem,
):
    dp = lax.axis_index("dp")
    t = lax.axis_index("tensor")
    here = {"z": dp // 4, "x": dp % 4, "y": t // 2, "c": t % 2}
    c = here["c"]

    def device(**moved):
        at = dict(here, **moved)
        return (at["z"] * 4 + at["x"], at["y"] * 2 + at["c"])

    def along(axis, k):
        return (here[axis] + k) % 4

    def tensor_peer(k):
        return (dp, (t + k) % 8)

    counter = [0]
    sent = []

    def remote(src, dst, to, at=None, start=True):
        i = counter[0] if at is None else at
        counter[0] += at is None
        copy = pltpu.make_async_remote_copy(
            src_ref=src,
            dst_ref=dst,
            send_sem=send_sem.at[i],
            recv_sem=recv_sem.at[i],
            device_id=to,
            device_id_type=MESH,
        )
        if start:
            copy.start()
        if at is None or not start:
            sent.append(copy)
        return copy

    sibling = device(c=1 - c)

    weights = []
    for i, (src, dst) in enumerate(
        ((wp_hbm, wp), (wg_hbm.at[0], wg), (wu_hbm.at[0], wu), (wd_hbm.at[0], wd))
    ):
        weights.append(pltpu.make_async_copy(src, dst, w_sem.at[i]))
        weights[-1].start()

    barrier = pltpu.get_barrier_semaphore()
    peers = [tensor_peer(k) for k in range(1, 8)]
    for axis in ("x", "z"):
        for k in (1, 2, 3):
            for core in (0, 1):
                peers.append(device(**{axis: along(axis, k), "c": core}))
    for peer in peers:
        pl.semaphore_signal(barrier, inc=1, device_id=peer, device_id_type=MESH)
    pl.semaphore_wait(barrier, len(peers))

    own_rows = pl.ds(pl.multiple_of(c * 8, 8), 8)
    other_rows = pl.ds(pl.multiple_of((1 - c) * 8, 8), 8)
    own_cols = pl.ds(pl.multiple_of(c * HALF, HALF), HALF)
    other_cols = pl.ds(pl.multiple_of((1 - c) * HALF, HALF), HALF)
    hidden[own_rows, :] = res_ref[:, own_cols].astype(F32)
    fin_s[0] = res_ref[:, other_cols].astype(F32)
    res_copy = remote(fin_s.at[0], hidden.at[own_rows, :], sibling)

    gw = gw_ref[...]
    route = (gw / jnp.sum(gw, axis=1, keepdims=True)).astype(BF16)
    put = iota((8, 128), 1) - iota((8, 128), 0) - t * 16
    ids = ids_ref[...].astype(F32).astype(BF16)
    table = dot(ids, (put == 0).astype(F32).astype(BF16)) + dot(
        route, (put == 8).astype(F32).astype(BF16)
    )
    z, x, y = here["z"], here["x"], here["y"]
    table_s[...] = table
    spread = [remote(table_s, table_r.at[k], tensor_peer(k)) for k in range(1, 8)]

    scaling = 128.0**-0.5
    first = (t == 0).astype(F32)
    shuffle = (iota((128, 128), 1) == (iota((128, 128), 0) % 8) * 16 + iota((128, 128), 0) // 8)
    shuffle = shuffle.astype(F32).astype(BF16)
    lane_row = iota((1, 256), 1) // 32
    lane_pos = iota((1, 256), 1) % 32 + t * 32
    own_block = (iota((128, 256), 0) % 8) == (iota((128, 256), 1) // 32)
    ones = jnp.ones((256, 128), BF16)
    lane = iota((8, 128), 1)
    stat[...] = jnp.zeros_like(stat)

    chunk_base = counter[0]
    counter[0] += 4 * 7

    def send_chunk(chunk, start=True):
        copies = []
        for i, k in enumerate((4, 3, 5, 2, 6, 1, 7)):
            to = (t + k) % 8
            copies.append(
                remote(
                    num_b.at[chunk, pl.ds(to * 4, 4)],
                    rec_num.at[k, chunk],
                    (dp, to),
                    at=chunk_base + chunk * 7 + i,
                    start=start,
                )
            )
        return copies

    def attend(blk, lower):
        at = pl.multiple_of(blk * 8, 8)
        rows = pl.ds(at, 8)
        limit = jnp.zeros((1, 256), jnp.int32)
        for r in range(8):
            limit = jnp.where(lane_row == r, len_ref[at + r], limit)
        bias = jnp.where(lane_pos < limit, 0.0, LOW)
        stats = jnp.zeros((8, 128), F32)
        for kv in range(2):
            q = q_ref[rows, pl.ds(kv * 16, 16), :].astype(F32).reshape(128, 128)
            q = q * lax.rsqrt(jnp.mean(q * q, axis=1, keepdims=True) + EPS) * qg_ref[...]
            q = dot(shuffle, q.astype(BF16)).astype(BF16)
            nk = nk_ref[rows, kv, :].astype(F32)
            nk = nk * lax.rsqrt(jnp.mean(nk * nk, axis=1, keepdims=True) + EPS) * kg_ref[...]
            nk = nk.astype(BF16).astype(F32)
            nv = nv_ref[rows, kv, :].astype(F32)
            keys = kc_ref[rows, kv].reshape(256, 128)
            values = vc_ref[rows, kv].reshape(256, 128)
            score = lax.dot_general(
                q, keys, (((1,), (1,)), ((), ())), preferred_element_type=F32
            )
            score = jnp.where(own_block, score * scaling + bias, LOW)
            fresh = (q.astype(F32).reshape(16, 8, 128) * nk[None]).reshape(128, 128)
            fresh = jnp.sum(fresh, axis=1, keepdims=True) * scaling
            top = jnp.maximum(jnp.max(score, axis=1, keepdims=True), fresh)
            weight = jnp.exp(score - top).astype(BF16)
            new_weight = jnp.exp(fresh - top).astype(BF16).astype(F32) * first
            number = dot(weight, values)
            total = dot(weight, ones) + new_weight
            number = number.reshape(16, 8, 128) + new_weight.reshape(16, 8, 1) * nv[None]
            top = jnp.broadcast_to(top, (128, 128)).reshape(16, 8, 128)
            total = total.reshape(16, 8, 128)
            for i in range(16):
                head = kv * 16 + i
                num_f[head, lower : lower + 8, :] = number[i]
                column = 8 * (head // 4) + head % 4
                stats = jnp.where(lane == column, top[i], stats)
                stats = jnp.where(lane == column + 4, total[i], stats)
        stat[rows, :] = stats

    def attend_chunk(chunk, carry):
        attend(chunk * 2, 0)
        attend(chunk * 2 + 1, 8)
        num_b[chunk] = num_f[...].astype(BF16)
        send_chunk(chunk)
        return carry

    lax.fori_loop(0, 4, attend_chunk, 0)
    stat_t[...] = stat[...].T
    partials = []
    for k in (4, 3, 5, 2, 6, 1, 7):
        to = (t + k) % 8
        tile = pl.ds(pl.multiple_of(to * 8, 8), 8)
        partials.append(remote(stat_t.at[tile, :], rec_stat.at[k], (dp, to)))
    for chunk in range(4):
        partials += send_chunk(chunk, start=False)

    for copy in spread:
        copy.wait_recv()
    table = table_s[...]
    for k in range(1, 8):
        table = table + table_r[k]
    packed[z, x] = table
    spread = [
        remote(packed.at[z, x], packed.at[z, x], device(x=along("x", k))) for k in (1, 2, 3)
    ]
    for chunk in range(4):
        rec_num[0, chunk] = num_b[chunk, pl.ds(t * 4, 4)]
    rec_stat[0] = stat_t[pl.ds(pl.multiple_of(t * 8, 8), 8), :]
    row = iota((384, 384), 0)
    col = iota((384, 384), 1)
    zz, yy, xx, rest = row // 96, (row // 24) % 4, (row // 6) % 4, row % 6
    perm[0] = (col == xx * 96 + zz * 24 + yy * 6 + rest).astype(F32).astype(BF16)
    perm[1] = (col == yy * 96 + xx * 24 + zz * 6 + rest).astype(F32).astype(BF16)
    zz, yy, xx, rest = col // 96, (col // 24) % 4, (col // 6) % 4, col % 6
    perm_t[0] = (row == xx * 96 + zz * 24 + yy * 6 + rest).astype(F32).astype(BF16)
    perm_t[1] = (row == yy * 96 + xx * 24 + zz * 6 + rest).astype(F32).astype(BF16)

    for copy in partials:
        copy.wait_recv()
    for copy in spread:
        copy.wait_recv()
    spread = [remote(packed.at[z], packed.at[z], device(z=along("z", k))) for k in (1, 2, 3)]
    tops = [rec_stat[k][0:4] for k in range(8)]
    best = tops[0]
    for top in tops[1:]:
        best = jnp.maximum(best, top)
    scale = [jnp.exp(top - best) for top in tops]
    whole = scale[0] * rec_stat[0][4:8]
    for k in range(1, 8):
        whole = whole + scale[k] * rec_stat[k][4:8]
    coef[...] = jnp.zeros_like(coef)
    for k in range(8):
        coef[8 * k : 8 * k + 4, :] = scale[k] / whole
    columns = coef[...].T
    for j in range(4):
        out = jnp.zeros((64, 128), F32)
        for k in range(8):
            out = out + columns[0:64, 8 * k + j : 8 * k + j + 1] * rec_num[k, :, j].reshape(64, 128).astype(F32)
        attn[:, 128 * j : 128 * j + 128] = out.astype(BF16)

    weights[0].wait()
    pairs = []
    for j in (0, 1):
        for tile in (0, 1):
            cols = pl.ds(pl.multiple_of((1 - c) * HALF + j * 1024 + tile * 512, 512), 512)
            pair_s[j, :, tile * 512 : tile * 512 + 512] = dot(attn[...], wp[:, cols]).astype(BF16)
        pairs.append(remote(pair_s.at[j], pair_r.at[j], sibling))
    shares = []
    for j in (0, 1):
        for tile in (0, 1):
            cols = pl.ds(pl.multiple_of(c * HALF + j * 1024 + tile * 512, 512), 512)
            part = dot(attn[...], wp[:, cols])
            if tile == 0:
                pairs[j].wait_recv()
            at = slice(tile * 512, tile * 512 + 512)
            send_b[j, :, at] = (part + pair_r[j, :, at].astype(F32)).astype(BF16)
        for k in (2, 1, 3):
            to = along("y", k)
            rows = pl.ds(pl.multiple_of(to * 16, 16), 16)
            shares.append(remote(send_b.at[j, rows, :], rec_b.at[k, j], device(y=to)))

    for copy in spread:
        copy.wait_recv()
    for tile in range(8):
        for iz in range(4):
            for ix in range(4):
                rows8 = packed[iz, ix]
                if tile > 0:
                    rows8 = pltpu.roll(rows8, 128 - 16 * tile, 1)
                meta[iz, ix, tile // 2, tile % 2] = rows8
    before = iota((256, 256), 0)
    after = iota((256, 256), 1)
    earlier = ((before // 8 == after // 8) & (before < after)).astype(F32).astype(BF16)
    slot_base = ((iota((1, 256), 1) // 8) * 3).astype(F32)
    slot_id = iota((SLOTS, 256), 0).astype(F32)
    for p in range(3):
        a, b, last = ORDER[p]
        for ib in range(4):
            for ia in range(4):
                at = dict(here, **{a: ia, b: ib})
                plane_meta[pl.ds((ib * 4 + ia) * 16, 16), :] = meta[
                    at["z"], at["x"], at["y"]
                ].reshape(16, 128)
        table = plane_meta[...].T
        chosen, gates = table[0:8], table[8:16]
        for k in range(4):
            for core in range(2):
                at = dict(here, **{last: k, "c": core})
                expert = (at["z"] * 32 + at["x"] * 8 + at["y"] * 2 + at["c"]).astype(F32)
                hit = (chosen == expert).astype(F32)
                used = jnp.sum(hit, axis=0, keepdims=True)
                gate = jnp.sum(hit * gates, axis=0, keepdims=True)
                rank = dot(jnp.broadcast_to(used, (8, 256)).astype(BF16), earlier)[0:1]
                slot = jnp.where(used > 0.5, slot_base + rank, -1.0)
                match = slot == slot_id
                first_slot = (k * 2 + core) * SLOTS
                disp[p, first_slot : first_slot + SLOTS, :] = match.astype(F32).astype(BF16)
                comb[p, first_slot : first_slot + SLOTS, :] = jnp.where(match, gate, 0.0).astype(BF16)

    res_copy.wait_recv()
    for copy in shares:
        copy.wait_recv()
    rows = pl.ds(pl.multiple_of(y * 16, 16), 16)
    for j in (0, 1):
        total = send_b[j, rows, :].astype(F32)
        for k in (1, 2, 3):
            total = total + rec_b[k, j].astype(F32)
        at = slice(j * 1024, j * 1024 + 1024)
        hidden[:, at] = hidden[:, at] + total
    value = hidden[...]
    squares = jnp.sum(value * value, axis=1, keepdims=True)
    sq_own[...] = jnp.broadcast_to(squares, (16, 128))
    sq_copy = remote(sq_own, sq_rec, sibling)
    sq_copy.wait_recv()
    mean = (squares + sq_rec[:, 0:1]) * (1.0 / D)
    normed = (value * lax.rsqrt(mean + EPS) * ng_ref[:, own_cols]).astype(BF16)

    stage = {}
    for wave in FORTH:
        for p in wave:
            order, first, width = PARTS[p]
            a, b, last = ORDER[order]
            g[p][here[b], here[a]] = normed[:, first : first + width]
            unit = g[p].at[here[b], here[a]]
            stage[p] = [remote(unit, unit, device(**{a: along(a, k)})) for k in (2, 1, 3)]
    for wave in FORTH:
        for p in wave:
            a, b, last = ORDER[PARTS[p][0]]
            for copy in stage[p]:
                copy.wait_recv()
            unit = g[p].at[here[b]]
            stage[p] = [remote(unit, unit, device(**{b: along(b, k)})) for k in (2, 1, 3)]
    locals_in = {}
    for wave in FORTH:
        for p in wave:
            order, first, width = PARTS[p]
            a, b, last = ORDER[order]
            for copy in stage[p]:
                copy.wait_recv()
            plane = g[p][...].reshape(256, width)
            stage[p] = []
            for k in (2, 1, 3, 0):
                to = along(last, k)
                wanted = pl.ds(pl.multiple_of(to * 2 * SLOTS, 2 * SLOTS), 2 * SLOTS)
                picked = dot(disp[order, wanted, :], plane)
                xs[p][k] = picked.astype(BF16).reshape(2, SLOTS, width)
                for j in (1, 0):
                    core = (c + j) % 2
                    src = xs[p].at[k, core]
                    dst = xr[p].at[c, here[last]]
                    if k == 0 and j == 0:
                        local = pltpu.make_async_copy(src, dst, loc_sem.at[p])
                        local.start()
                        locals_in[p] = local
                    else:
                        stage[p].append(remote(src, dst, device(**{last: to, "c": core})))
    for n, wave in enumerate(FORTH):
        for p in wave:
            order, first, width = PARTS[p]
            for copy in stage[p]:
                copy.wait_recv()
            locals_in[p].wait()
            for half in (0, 1):
                block = xr[p][half].reshape(384, width)
                if order > 0:
                    block = dot(perm[order - 1], block).astype(BF16)
                x_full[:, half * HALF + first : half * HALF + first + width] = block
        if n == 0:
            for copy in weights[1:]:
                copy.wait()
        low = min(PARTS[p][1] for p in wave)
        high = max(PARTS[p][1] + PARTS[p][2] for p in wave)

        def expert(i, carry, n=n, low=low, high=high):
            cols = pl.ds(pl.multiple_of(i * 256, 256), 256)
            sums = []
            for which, weight in ((0, wg), (1, wu)):
                total = dot(x_full[:, low:high], weight[low:high, cols])
                total = total + dot(
                    x_full[:, HALF + low : HALF + high], weight[HALF + low : HALF + high, cols]
                )
                if n > 0:
                    total = total + acc[which, :, cols]
                if n < len(FORTH) - 1:
                    acc[which, :, cols] = total
                sums.append(total)
            if n == len(FORTH) - 1:
                gate, up = sums
                act[:, cols] = (gate / (1.0 + jnp.exp(-gate)) * up).astype(BF16)
            return carry

        lax.fori_loop(0, FFW // 256, expert, 0)

    stage, locals_out, ready = {}, {}, []
    for wave in BACK:
        for p in wave:
            order, first, width = PARTS[p]
            a, b, last = ORDER[order]
            if order == 0:
                turned = act
            else:
                turned = act_p.at[order - 1]
                if order not in ready:
                    ready.append(order)
                    turned[...] = dot(perm_t[order - 1], act[...]).astype(BF16)
            stage[p] = []
            for j in (1, 0):
                core = (c + j) % 2
                cols = pl.ds(pl.multiple_of(core * HALF + first, 128), width)
                result = dot(turned[...], wd[:, cols])
                ys[p][j] = result.astype(BF16).reshape(4, SLOTS, width)
                for k in (2, 1, 3, 0):
                    to = along(last, k)
                    src = ys[p].at[j, to]
                    dst = yr[p].at[here[last] * 2 + c]
                    if k == 0 and j == 0:
                        local = pltpu.make_async_copy(src, dst, loc_sem.at[len(PARTS) + p])
                        local.start()
                        locals_out[p] = local
                    else:
                        stage[p].append(remote(src, dst, device(**{last: to, "c": core})))
    for wave in BACK:
        for p in wave:
            order, first, width = PARTS[p]
            a, b, last = ORDER[order]
            for copy in stage[p]:
                copy.wait_recv()
            locals_out[p].wait()
            summed = lax.dot_general(
                comb[order], yr[p][...].reshape(8 * SLOTS, width), (((0,), (0,)), ((), ())),
                preferred_element_type=F32,
            )
            ps[p][...] = summed.astype(BF16).reshape(4, 64, width)
            stage[p] = []
            for k in (2, 1, 3):
                to = along(b, k)
                stage[p].append(remote(ps[p].at[to], rb[p].at[k], device(**{b: to})))
        for p in wave:
            order, first, width = PARTS[p]
            a, b, last = ORDER[order]
            for copy in stage[p]:
                copy.wait_recv()
            total = ps[p][here[b]].astype(F32)
            for k in (1, 2, 3):
                total = total + rb[p][k].astype(F32)
            ra_s[p][...] = total.astype(BF16).reshape(4, 16, width)
            stage[p] = []
            for k in (2, 1, 3):
                to = along(a, k)
                stage[p].append(remote(ra_s[p].at[to], ra_r[p].at[k], device(**{a: to})))
    for wave in BACK:
        for p in wave:
            order, first, width = PARTS[p]
            a, b, last = ORDER[order]
            for copy in stage[p]:
                copy.wait_recv()
            total = ra_s[p][here[a]].astype(F32)
            for k in (1, 2, 3):
                total = total + ra_r[p][k].astype(F32)
            cols = slice(first, first + width)
            hidden[:, cols] = hidden[:, cols] + total

    fin_s[1] = hidden[other_rows, :]
    fin = remote(fin_s.at[1], fin_r, sibling)
    out_ref[:, own_cols] = hidden[own_rows, :].astype(BF16)
    fin.wait_recv()
    out_ref[:, other_cols] = fin_r[...].astype(BF16)
    for copy in sent:
        copy.wait_send()


COPIES = 1 + 7 + 28 + 7 + 3 + 3 + 2 + 6 + 1 + 1 + len(PARTS) * (3 + 3 + 7 + 7 + 3 + 3)


def shards(
    queries, new_keys, new_values, key_cache, value_cache, lengths, residual_in, query_gain, key_gain,
    out_proj, norm_gain, expert_ids, gate_weights, expert_gate, expert_up, expert_down,
):
    vmem = pl.BlockSpec(memory_space=pltpu.VMEM)
    anywhere = pl.BlockSpec(memory_space=pl.ANY)

    def each(shape_of):
        return [VMEM(shape_of(width), BF16) for _, _, width in PARTS]

    return pl.pallas_call(
        kernel,
        out_shape=jax.ShapeDtypeStruct((8, D), BF16),
        in_specs=[vmem] * 5 + [pl.BlockSpec(memory_space=pltpu.SMEM)] + [vmem] * 6 + [anywhere] * 4,
        out_specs=vmem,
        scratch_shapes=[
            VMEM((512, D), BF16), VMEM((D, FFW), BF16), VMEM((D, FFW), BF16), VMEM((FFW, D), BF16),
            VMEM((32, 16, 128), F32), VMEM((4, 32, 16, 128), BF16), VMEM((128, 128), F32),
            VMEM((128, 128), F32), VMEM((128, 128), F32), VMEM((8, 4, 4, 16, 128), BF16),
            VMEM((8, 8, 128), F32), VMEM((64, 512), BF16),
            VMEM((2, 64, 1024), BF16), VMEM((2, 64, 1024), BF16), VMEM((2, 64, 1024), BF16),
            VMEM((4, 2, 16, 1024), BF16), VMEM((16, HALF), F32),
            VMEM((16, 128), F32), VMEM((16, 128), F32),
            VMEM((8, 128), F32), VMEM((8, 8, 128), F32), VMEM((4, 4, 8, 128), F32),
            VMEM((4, 4, 4, 2, 8, 128), F32), VMEM((256, 128), F32),
            VMEM((3, 8 * SLOTS, 256), BF16), VMEM((3, 8 * SLOTS, 256), BF16),
            VMEM((384, D), BF16), VMEM((2, 384, 384), BF16), VMEM((2, 384, 384), BF16),
            VMEM((2, 384, FFW), F32), VMEM((384, FFW), BF16), VMEM((2, 384, FFW), BF16),
            each(lambda w: (4, 4, 16, w)),
            each(lambda w: (4, 2, SLOTS, w)),
            each(lambda w: (2, 4, SLOTS, w)),
            each(lambda w: (2, 4, SLOTS, w)),
            each(lambda w: (8, SLOTS, w)),
            each(lambda w: (4, 64, w)), each(lambda w: (4, 64, w)),
            each(lambda w: (4, 16, w)), each(lambda w: (4, 16, w)),
            VMEM((2, 8, HALF), F32), VMEM((8, HALF), F32),
            pltpu.SemaphoreType.DMA((4,)), pltpu.SemaphoreType.DMA((2 * len(PARTS),)),
            pltpu.SemaphoreType.DMA((COPIES,)), pltpu.SemaphoreType.DMA((COPIES,)),
        ],
        compiler_params=pltpu.CompilerParams(
            collective_id=0, has_side_effects=True, vmem_limit_bytes=60 * 2**20
        ),
        cost_estimate=pl.CostEstimate(flops=10**10, bytes_accessed=26 * 2**20, transcendentals=10**6),
    )(
        queries, new_keys, new_values, key_cache, value_cache, lengths, residual_in,
        query_gain.reshape(1, 128), key_gain.reshape(1, 128), norm_gain.reshape(1, D),
        expert_ids, gate_weights, out_proj, expert_gate, expert_up, expert_down,
    )


def solution(mesh):
    rows = P(("dp", "tensor"), None)
    experts = P(("dp", "tensor"), None, None)
    cache = P("dp", None, "tensor", None)
    heads = P("dp", None, None)
    return jax.shard_map(
        shards,
        mesh=mesh,
        in_specs=(
            heads, heads, heads, cache, cache, P("dp"), rows, P(), P(),
            P("tensor", None), P(), rows, rows, experts, experts, experts,
        ),
        out_specs=rows,
        check_vma=False,
    )
```

time: 107 us -> 91 us (0.85)
  Pallas kernels: 104 us -> 89.4 us
  local copies, waits for them, and re-layouts: 2.81 us -> 1.47 us
    pallas_call x1, Pallas kernels: 104 us -> 89.4 us  [shards(): pl.pallas_call(kernel, out_shape=jax.ShapeDtypeStruct((8, D), BF16), in_s...]
    reshape x1 -> x0, local copies, waits for them, and re-layouts: 1.33 us -> none  [shards(): norm_gain.reshape(2, HALF)]
where the time goes in v2:
time: 91 us; the launch traced here: 90.8 us
  Pallas kernels  89.4 us (98%)
  local copies, waits for them, and re-layouts  1.47 us (2%)
    pallas_call x1, Pallas kernels, shards(): pl.pallas_call(kernel, out_shape=jax.ShapeDtypeStruct((8, D), BF16), in_s...  89.4 us

profile of v2, /device:TPU:1, one launch (start us, length us, event | category | flops | bytes accessed | tf_op | source)
XLA Modules:
  0.0 90.8 jit_solution(2382240638345496872)
XLA Ops:
  0.0 89.4 %shard_map.154 = bf16[8,4096]{1,0:T(8,128)(2,1)} custom-call(bf16[64,32,128]{2,1,0:T(8,128)(2,1)} %q_ref.1, bf16[64,2,128]{2,1,0:T(2,128)(2,1)} %nk_ref.1, bf16[64,2,128]{2,1,0:T(2,128)(2,1)} %nv_ref.1, bf16[64,2,32,128]{3,2,1,0:T(8,128)(2,1)} %kc_ref.1, bf16[64,2,32,128]{3,2,1,0:T(8,128)(2,1)} %vc_ref.1, s32[64]{0:T(128)} %len_ref.1, ...), custom_call_target="tpu_custom_call" | custom-call | flops 10000000000 | bytes 27262976 | tf_op jit(solution)/shard_map/pallas_call | solution.py:494
  89.4 1.5 %copy.18 = bf16[8,4096]{1,0:T(8,128)(2,1)} copy(bf16[8,4096]{1,0:T(8,128)(2,1)} %shard_map.154) | data formatting | bytes 131072

commit v3 on v2

--- a/solution.py
+++ b/solution.py
@@ -32,9 +32,10 @@
 
 
 def kernel(
-    q_ref, nk_ref, nv_ref, kc_ref, vc_ref, len_ref, res_ref, qg_ref, kg_ref, ng_ref, ids_ref, gw_ref,
+    q_hbm, nk_hbm, nv_hbm, kc_hbm, vc_hbm, len_hbm, res_hbm, qg_hbm, kg_hbm, ng_hbm, ids_hbm, gw_hbm,
     wp_hbm, wg_hbm, wu_hbm, wd_hbm,
     out_ref,
+    q_ref, nk_ref, nv_ref, kc_ref, vc_ref, len_ref, res_ref, qg_ref, kg_ref, ng_ref, ids_ref, gw_ref,
     wp, wg, wu, wd,
     num_f, num_b, stat, stat_t, coef, rec_num, rec_stat, attn,
     pair_s, pair_r, send_b, rec_b, hidden, sq_own, sq_rec,
@@ -42,7 +43,7 @@
     x_full, perm, perm_t, acc, act, act_p,
     g, xs, xr, ys, yr, ps, rb, ra_s, ra_r,
     fin_s, fin_r,
-    w_sem, loc_sem, send_sem, recv_sem,
+    in_sem, w_sem, loc_sem, send_sem, recv_sem,
 ):
     dp = lax.axis_index("dp")
     t = lax.axis_index("tensor")
@@ -60,33 +61,44 @@
         return (dp, (t + k) % 8)
 
     counter = [0]
-    sent = []
-
-    def remote(src, dst, to, at=None, start=True):
-        i = counter[0] if at is None else at
-        counter[0] += at is None
-        copy = pltpu.make_async_remote_copy(
-            src_ref=src,
-            dst_ref=dst,
-            send_sem=send_sem.at[i],
-            recv_sem=recv_sem.at[i],
-            device_id=to,
-            device_id_type=MESH,
-        )
-        if start:
-            copy.start()
-        if at is None or not start:
-            sent.append(copy)
-        return copy
+    groups = []
+
+    class Group:
+        def __init__(self, like):
+            self.index = counter[0]
+            counter[0] += 1
+            self.like = like
+            groups.append(self)
+
+        def copy(self, src, dst, to):
+            return pltpu.make_async_remote_copy(
+                src_ref=src,
+                dst_ref=dst,
+                send_sem=send_sem.at[self.index],
+                recv_sem=recv_sem.at[self.index],
+                device_id=to,
+                device_id_type=MESH,
+            )
+
+        def send(self, src, dst, to):
+            self.copy(src, dst, to).start()
+
+        def wait_recv(self):
+            self.copy(self.like, self.like, sibling).wait_recv()
+
+        def wait_send(self):
+            self.copy(self.like, self.like, sibling).wait_send()
+
+    def remote(src, dst, to):
+        group = Group(src)
+        group.send(src, dst, to)
+        return group
 
     sibling = device(c=1 - c)
-
-    weights = []
-    for i, (src, dst) in enumerate(
-        ((wp_hbm, wp), (wg_hbm.at[0], wg), (wu_hbm.at[0], wu), (wd_hbm.at[0], wd))
-    ):
-        weights.append(pltpu.make_async_copy(src, dst, w_sem.at[i]))
-        weights[-1].start()
+    own_rows = pl.ds(pl.multiple_of(c * 8, 8), 8)
+    other_rows = pl.ds(pl.multiple_of((1 - c) * 8, 8), 8)
+    own_cols = pl.ds(pl.multiple_of(c * HALF, HALF), HALF)
+    other_cols = pl.ds(pl.multiple_of((1 - c) * HALF, HALF), HALF)
 
     barrier = pltpu.get_barrier_semaphore()
     peers = [tensor_peer(k) for k in range(1, 8)]
@@ -96,27 +108,17 @@
                 peers.append(device(**{axis: along(axis, k), "c": core}))
     for peer in peers:
         pl.semaphore_signal(barrier, inc=1, device_id=peer, device_id_type=MESH)
-    pl.semaphore_wait(barrier, len(peers))
-
-    own_rows = pl.ds(pl.multiple_of(c * 8, 8), 8)
-    other_rows = pl.ds(pl.multiple_of((1 - c) * 8, 8), 8)
-    own_cols = pl.ds(pl.multiple_of(c * HALF, HALF), HALF)
-    other_cols = pl.ds(pl.multiple_of((1 - c) * HALF, HALF), HALF)
-    hidden[own_rows, :] = res_ref[:, own_cols].astype(F32)
-    fin_s[0] = res_ref[:, other_cols].astype(F32)
-    res_copy = remote(fin_s.at[0], hidden.at[own_rows, :], sibling)
-
-    gw = gw_ref[...]
-    route = (gw / jnp.sum(gw, axis=1, keepdims=True)).astype(BF16)
-    put = iota((8, 128), 1) - iota((8, 128), 0) - t * 16
-    ids = ids_ref[...].astype(F32).astype(BF16)
-    table = dot(ids, (put == 0).astype(F32).astype(BF16)) + dot(
-        route, (put == 8).astype(F32).astype(BF16)
-    )
-    z, x, y = here["z"], here["x"], here["y"]
-    table_s[...] = table
-    spread = [remote(table_s, table_r.at[k], tensor_peer(k)) for k in range(1, 8)]
-
+
+    inputs = []
+    for i, (src, dst) in enumerate(
+        (
+            (q_hbm, q_ref), (kc_hbm, kc_ref), (vc_hbm, vc_ref), (nk_hbm, nk_ref), (nv_hbm, nv_ref),
+            (len_hbm, len_ref), (qg_hbm, qg_ref), (kg_hbm, kg_ref), (ids_hbm, ids_ref),
+            (gw_hbm, gw_ref), (res_hbm, res_ref), (ng_hbm, ng_ref),
+        )
+    ):
+        inputs.append(pltpu.make_async_copy(src, dst, in_sem.at[i]))
+        inputs[-1].start()
     scaling = 128.0**-0.5
     first = (t == 0).astype(F32)
     shuffle = (iota((128, 128), 1) == (iota((128, 128), 0) % 8) * 16 + iota((128, 128), 0) // 8)
@@ -128,23 +130,12 @@
     lane = iota((8, 128), 1)
     stat[...] = jnp.zeros_like(stat)
 
-    chunk_base = counter[0]
-    counter[0] += 4 * 7
-
-    def send_chunk(chunk, start=True):
-        copies = []
-        for i, k in enumerate((4, 3, 5, 2, 6, 1, 7)):
+    shares_a = Group(rec_num.at[pl.ds(1, 7)])
+
+    def send_chunk(chunk):
+        for k in (4, 3, 5, 2, 6, 1, 7):
             to = (t + k) % 8
-            copies.append(
-                remote(
-                    num_b.at[chunk, pl.ds(to * 4, 4)],
-                    rec_num.at[k, chunk],
-                    (dp, to),
-                    at=chunk_base + chunk * 7 + i,
-                    start=start,
-                )
-            )
-        return copies
+            shares_a.send(num_b.at[chunk, pl.ds(to * 4, 4)], rec_num.at[k, chunk], (dp, to))
 
     def attend(blk, lower):
         at = pl.multiple_of(blk * 8, 8)
@@ -186,35 +177,65 @@
                 stats = jnp.where(lane == column + 4, total[i], stats)
         stat[rows, :] = stats
 
-    def attend_chunk(chunk, carry):
+    def attend_chunk(chunk):
         attend(chunk * 2, 0)
         attend(chunk * 2 + 1, 8)
         num_b[chunk] = num_f[...].astype(BF16)
+
+    for copy in inputs[:8]:
+        copy.wait()
+    weights = [pltpu.make_async_copy(wp_hbm, wp, w_sem.at[0])]
+    weights[0].start()
+    attend_chunk(0)
+    pl.semaphore_wait(barrier, len(peers))
+    send_chunk(0)
+
+    for copy in inputs[8:]:
+        copy.wait()
+    gw = gw_ref[...]
+    route = (gw / jnp.sum(gw, axis=1, keepdims=True)).astype(BF16)
+    put = iota((8, 128), 1) - iota((8, 128), 0) - t * 16
+    ids = ids_ref[...].astype(F32).astype(BF16)
+    table = dot(ids, (put == 0).astype(F32).astype(BF16)) + dot(
+        route, (put == 8).astype(F32).astype(BF16)
+    )
+    z, x, y = here["z"], here["x"], here["y"]
+    table_s[...] = table
+    spread = Group(table_r.at[pl.ds(1, 7)])
+    for k in range(1, 8):
+        spread.send(table_s, table_r.at[k], tensor_peer(k))
+
+    hidden[own_rows, :] = res_ref[:, own_cols].astype(F32)
+    fin_s[0] = res_ref[:, other_cols].astype(F32)
+    res_copy = remote(fin_s.at[0], hidden.at[own_rows, :], sibling)
+
+    def attend_more(chunk, carry):
+        attend_chunk(chunk)
         send_chunk(chunk)
         return carry
 
-    lax.fori_loop(0, 4, attend_chunk, 0)
+    lax.fori_loop(1, 4, attend_more, 0)
     stat_t[...] = stat[...].T
-    partials = []
+    tops_a = Group(rec_stat.at[pl.ds(1, 7)])
     for k in (4, 3, 5, 2, 6, 1, 7):
         to = (t + k) % 8
         tile = pl.ds(pl.multiple_of(to * 8, 8), 8)
-        partials.append(remote(stat_t.at[tile, :], rec_stat.at[k], (dp, to)))
-    for chunk in range(4):
-        partials += send_chunk(chunk, start=False)
-
-    for copy in spread:
-        copy.wait_recv()
+        tops_a.send(stat_t.at[tile, :], rec_stat.at[k], (dp, to))
+
+    spread.wait_recv()
     table = table_s[...]
     for k in range(1, 8):
         table = table + table_r[k]
     packed[z, x] = table
-    spread = [
-        remote(packed.at[z, x], packed.at[z, x], device(x=along("x", k))) for k in (1, 2, 3)
-    ]
+    spread = Group(packed.at[z, pl.ds(0, 3)])
+    for k in (1, 2, 3):
+        spread.send(packed.at[z, x], packed.at[z, x], device(x=along("x", k)))
     for chunk in range(4):
         rec_num[0, chunk] = num_b[chunk, pl.ds(t * 4, 4)]
     rec_stat[0] = stat_t[pl.ds(pl.multiple_of(t * 8, 8), 8), :]
+    for i, (src, dst) in enumerate(((wg_hbm, wg), (wu_hbm, wu), (wd_hbm, wd))):
+        weights.append(pltpu.make_async_copy(src.at[0], dst, w_sem.at[1 + i]))
+        weights[-1].start()
     row = iota((384, 384), 0)
     col = iota((384, 384), 1)
     zz, yy, xx, rest = row // 96, (row // 24) % 4, (row // 6) % 4, row % 6
@@ -224,11 +245,12 @@
     perm_t[0] = (row == xx * 96 + zz * 24 + yy * 6 + rest).astype(F32).astype(BF16)
     perm_t[1] = (row == yy * 96 + xx * 24 + zz * 6 + rest).astype(F32).astype(BF16)
 
-    for copy in partials:
-        copy.wait_recv()
-    for copy in spread:
-        copy.wait_recv()
-    spread = [remote(packed.at[z], packed.at[z], device(z=along("z", k))) for k in (1, 2, 3)]
+    tops_a.wait_recv()
+    shares_a.wait_recv()
+    spread.wait_recv()
+    spread = Group(packed.at[pl.ds(0, 3)])
+    for k in (1, 2, 3):
+        spread.send(packed.at[z], packed.at[z], device(z=along("z", k)))
     tops = [rec_stat[k][0:4] for k in range(8)]
     best = tops[0]
     for top in tops[1:]:
@@ -254,7 +276,7 @@
             cols = pl.ds(pl.multiple_of((1 - c) * HALF + j * 1024 + tile * 512, 512), 512)
             pair_s[j, :, tile * 512 : tile * 512 + 512] = dot(attn[...], wp[:, cols]).astype(BF16)
         pairs.append(remote(pair_s.at[j], pair_r.at[j], sibling))
-    shares = []
+    shares = Group(rec_b.at[pl.ds(1, 3)])
     for j in (0, 1):
         for tile in (0, 1):
             cols = pl.ds(pl.multiple_of(c * HALF + j * 1024 + tile * 512, 512), 512)
@@ -266,10 +288,9 @@
         for k in (2, 1, 3):
             to = along("y", k)
             rows = pl.ds(pl.multiple_of(to * 16, 16), 16)
-            shares.append(remote(send_b.at[j, rows, :], rec_b.at[k, j], device(y=to)))
-
-    for copy in spread:
-        copy.wait_recv()
+            shares.send(send_b.at[j, rows, :], rec_b.at[k, j], device(y=to))
+
+    spread.wait_recv()
     for tile in range(8):
         for iz in range(4):
             for ix in range(4):
@@ -307,8 +328,7 @@
                 comb[p, first_slot : first_slot + SLOTS, :] = jnp.where(match, gate, 0.0).astype(BF16)
 
     res_copy.wait_recv()
-    for copy in shares:
-        copy.wait_recv()
+    shares.wait_recv()
     rows = pl.ds(pl.multiple_of(y * 16, 16), 16)
     for j in (0, 1):
         total = send_b[j, rows, :].astype(F32)
@@ -331,43 +351,44 @@
             a, b, last = ORDER[order]
             g[p][here[b], here[a]] = normed[:, first : first + width]
             unit = g[p].at[here[b], here[a]]
-            stage[p] = [remote(unit, unit, device(**{a: along(a, k)})) for k in (2, 1, 3)]
+            stage[p] = Group(g[p].at[here[b], pl.ds(0, 3)])
+            for k in (2, 1, 3):
+                stage[p].send(unit, unit, device(**{a: along(a, k)}))
     for wave in FORTH:
         for p in wave:
             a, b, last = ORDER[PARTS[p][0]]
-            for copy in stage[p]:
-                copy.wait_recv()
+            stage[p].wait_recv()
             unit = g[p].at[here[b]]
-            stage[p] = [remote(unit, unit, device(**{b: along(b, k)})) for k in (2, 1, 3)]
+            stage[p] = Group(g[p].at[pl.ds(0, 3)])
+            for k in (2, 1, 3):
+                stage[p].send(unit, unit, device(**{b: along(b, k)}))
     locals_in = {}
     for wave in FORTH:
         for p in wave:
             order, first, width = PARTS[p]
             a, b, last = ORDER[order]
-            for copy in stage[p]:
-                copy.wait_recv()
+            stage[p].wait_recv()
             plane = g[p][...].reshape(256, width)
-            stage[p] = []
+            stage[p] = Group(xs[p].at[pl.ds(0, 7)])
             for k in (2, 1, 3, 0):
                 to = along(last, k)
                 wanted = pl.ds(pl.multiple_of(to * 2 * SLOTS, 2 * SLOTS), 2 * SLOTS)
                 picked = dot(disp[order, wanted, :], plane)
-                xs[p][k] = picked.astype(BF16).reshape(2, SLOTS, width)
+                xs[p][2 * k : 2 * k + 2] = picked.astype(BF16).reshape(2, SLOTS, width)
                 for j in (1, 0):
                     core = (c + j) % 2
-                    src = xs[p].at[k, core]
+                    src = xs[p].at[2 * k + core]
                     dst = xr[p].at[c, here[last]]
                     if k == 0 and j == 0:
                         local = pltpu.make_async_copy(src, dst, loc_sem.at[p])
                         local.start()
                         locals_in[p] = local
                     else:
-                        stage[p].append(remote(src, dst, device(**{last: to, "c": core})))
+                        stage[p].send(src, dst, device(**{last: to, "c": core}))
     for n, wave in enumerate(FORTH):
         for p in wave:
             order, first, width = PARTS[p]
-            for copy in stage[p]:
-                copy.wait_recv()
+            stage[p].wait_recv()
             locals_in[p].wait()
             for half in (0, 1):
                 block = xr[p][half].reshape(384, width)
@@ -412,57 +433,54 @@
                 if order not in ready:
                     ready.append(order)
                     turned[...] = dot(perm_t[order - 1], act[...]).astype(BF16)
-            stage[p] = []
+            stage[p] = Group(ys[p].at[pl.ds(0, 7)])
             for j in (1, 0):
                 core = (c + j) % 2
                 cols = pl.ds(pl.multiple_of(core * HALF + first, 128), width)
                 result = dot(turned[...], wd[:, cols])
-                ys[p][j] = result.astype(BF16).reshape(4, SLOTS, width)
+                ys[p][4 * j : 4 * j + 4] = result.astype(BF16).reshape(4, SLOTS, width)
                 for k in (2, 1, 3, 0):
                     to = along(last, k)
-                    src = ys[p].at[j, to]
+                    src = ys[p].at[4 * j + to]
                     dst = yr[p].at[here[last] * 2 + c]
                     if k == 0 and j == 0:
                         local = pltpu.make_async_copy(src, dst, loc_sem.at[len(PARTS) + p])
                         local.start()
                         locals_out[p] = local
                     else:
-                        stage[p].append(remote(src, dst, device(**{last: to, "c": core})))
+                        stage[p].send(src, dst, device(**{last: to, "c": core}))
     for wave in BACK:
         for p in wave:
             order, first, width = PARTS[p]
             a, b, last = ORDER[order]
-            for copy in stage[p]:
-                copy.wait_recv()
+            stage[p].wait_recv()
             locals_out[p].wait()
             summed = lax.dot_general(
                 comb[order], yr[p][...].reshape(8 * SLOTS, width), (((0,), (0,)), ((), ())),
                 preferred_element_type=F32,
             )
             ps[p][...] = summed.astype(BF16).reshape(4, 64, width)
-            stage[p] = []
+            stage[p] = Group(ps[p].at[pl.ds(0, 3)])
             for k in (2, 1, 3):
                 to = along(b, k)
-                stage[p].append(remote(ps[p].at[to], rb[p].at[k], device(**{b: to})))
+                stage[p].send(ps[p].at[to], rb[p].at[k], device(**{b: to}))
         for p in wave:
             order, first, width = PARTS[p]
             a, b, last = ORDER[order]
-            for copy in stage[p]:
-                copy.wait_recv()
+            stage[p].wait_recv()
             total = ps[p][here[b]].astype(F32)
             for k in (1, 2, 3):
                 total = total + rb[p][k].astype(F32)
             ra_s[p][...] = total.astype(BF16).reshape(4, 16, width)
-            stage[p] = []
+            stage[p] = Group(ra_s[p].at[pl.ds(0, 3)])
             for k in (2, 1, 3):
                 to = along(a, k)
-                stage[p].append(remote(ra_s[p].at[to], ra_r[p].at[k], device(**{a: to})))
+                stage[p].send(ra_s[p].at[to], ra_r[p].at[k], device(**{a: to}))
     for wave in BACK:
         for p in wave:
             order, first, width = PARTS[p]
             a, b, last = ORDER[order]
-            for copy in stage[p]:
-                copy.wait_recv()
+            stage[p].wait_recv()
             total = ra_s[p][here[a]].astype(F32)
             for k in (1, 2, 3):
                 total = total + ra_r[p][k].astype(F32)
@@ -474,18 +492,17 @@
     out_ref[:, own_cols] = hidden[own_rows, :].astype(BF16)
     fin.wait_recv()
     out_ref[:, other_cols] = fin_r[...].astype(BF16)
-    for copy in sent:
-        copy.wait_send()
-
-
-COPIES = 1 + 7 + 28 + 7 + 3 + 3 + 2 + 6 + 1 + 1 + len(PARTS) * (3 + 3 + 7 + 7 + 3 + 3)
+    for group in groups:
+        group.wait_send()
+
+
+GROUPS = 11 + 6 * len(PARTS)
 
 
 def shards(
     queries, new_keys, new_values, key_cache, value_cache, lengths, residual_in, query_gain, key_gain,
     out_proj, norm_gain, expert_ids, gate_weights, expert_gate, expert_up, expert_down,
 ):
-    vmem = pl.BlockSpec(memory_space=pltpu.VMEM)
     anywhere = pl.BlockSpec(memory_space=pl.ANY)
 
     def each(shape_of):
@@ -494,9 +511,13 @@
     return pl.pallas_call(
         kernel,
         out_shape=jax.ShapeDtypeStruct((8, D), BF16),
-        in_specs=[vmem] * 5 + [pl.BlockSpec(memory_space=pltpu.SMEM)] + [vmem] * 6 + [anywhere] * 4,
-        out_specs=vmem,
+        in_specs=[anywhere] * 16,
+        out_specs=pl.BlockSpec(memory_space=pltpu.VMEM),
         scratch_shapes=[
+            VMEM((64, 32, 128), BF16), VMEM((64, 2, 128), BF16), VMEM((64, 2, 128), BF16),
+            VMEM((64, 2, 32, 128), BF16), VMEM((64, 2, 32, 128), BF16), pltpu.SMEM((64,), jnp.int32),
+            VMEM((8, D), BF16), VMEM((1, 128), F32), VMEM((1, 128), F32), VMEM((1, D), F32),
+            VMEM((8, 8), jnp.int32), VMEM((8, 8), F32),
             VMEM((512, D), BF16), VMEM((D, FFW), BF16), VMEM((D, FFW), BF16), VMEM((FFW, D), BF16),
             VMEM((32, 16, 128), F32), VMEM((4, 32, 16, 128), BF16), VMEM((128, 128), F32),
             VMEM((128, 128), F32), VMEM((128, 128), F32), VMEM((8, 4, 4, 16, 128), BF16),
@@ -510,15 +531,15 @@
             VMEM((384, D), BF16), VMEM((2, 384, 384), BF16), VMEM((2, 384, 384), BF16),
             VMEM((2, 384, FFW), F32), VMEM((384, FFW), BF16), VMEM((2, 384, FFW), BF16),
             each(lambda w: (4, 4, 16, w)),
-            each(lambda w: (4, 2, SLOTS, w)),
+            each(lambda w: (8, SLOTS, w)),
             each(lambda w: (2, 4, SLOTS, w)),
-            each(lambda w: (2, 4, SLOTS, w)),
+            each(lambda w: (8, SLOTS, w)),
             each(lambda w: (8, SLOTS, w)),
             each(lambda w: (4, 64, w)), each(lambda w: (4, 64, w)),
             each(lambda w: (4, 16, w)), each(lambda w: (4, 16, w)),
             VMEM((2, 8, HALF), F32), VMEM((8, HALF), F32),
-            pltpu.SemaphoreType.DMA((4,)), pltpu.SemaphoreType.DMA((2 * len(PARTS),)),
-            pltpu.SemaphoreType.DMA((COPIES,)), pltpu.SemaphoreType.DMA((COPIES,)),
+            pltpu.SemaphoreType.DMA((12,)), pltpu.SemaphoreType.DMA((4,)), pltpu.SemaphoreType.DMA((2 * len(PARTS),)),
+            pltpu.SemaphoreType.DMA((GROUPS,)), pltpu.SemaphoreType.DMA((GROUPS,)),
         ],
         compiler_params=pltpu.CompilerParams(
             collective_id=0, has_side_effects=True, vmem_limit_bytes=60 * 2**20

time: 91 us -> 84.8 us (0.932)
  Pallas kernels: 89.4 us -> 83.2 us
    pallas_call x1, Pallas kernels: 89.4 us -> 83.2 us  [shards(): pl.pallas_call(kernel, out_shape=jax.ShapeDtypeStruct((8, D), BF16), in_s...]
where the time goes in v3:
time: 84.8 us; the launch traced here: 84.7 us
  Pallas kernels  83.2 us (98%)
  local copies, waits for them, and re-layouts  1.47 us (2%)
    pallas_call x1, Pallas kernels, shards(): pl.pallas_call(kernel, out_shape=jax.ShapeDtypeStruct((8, D), BF16), in_s...  83.2 us

profile of v3, /device:TPU:1, one launch (start us, length us, event | category | flops | bytes accessed | tf_op | source)
XLA Modules:
  0.0 84.7 jit_solution(14705176497000877755)
XLA Ops:
  0.0 83.2 %shard_map.154 = bf16[8,4096]{1,0:T(8,128)(2,1)} custom-call(bf16[64,32,128]{2,1,0:T(8,128)(2,1)} %q_hbm.1, bf16[64,2,128]{2,1,0:T(2,128)(2,1)} %nk_hbm.1, bf16[64,2,128]{2,1,0:T(2,128)(2,1)} %nv_hbm.1, bf16[64,2,32,128]{3,2,1,0:T(8,128)(2,1)} %kc_hbm.1, bf16[64,2,32,128]{3,2,1,0:T(8,128)(2,1)} %vc_hbm.1, s32[64]{0:T(128)} %len_hbm.1, ...), custom_call_target="tpu_custom_call" | custom-call | flops 10000000000 | bytes 27262976 | tf_op jit(solution)/shard_map/pallas_call | solution.py:511
  83.2 1.5 %copy.18 = bf16[8,4096]{1,0:T(8,128)(2,1)} copy(bf16[8,4096]{1,0:T(8,128)(2,1)} %shard_map.154) | data formatting | bytes 131072

commit v4 on v3

--- a/solution.py
+++ b/solution.py
@@ -17,10 +17,13 @@
 EPS = 1e-6
 LOW = -1e30
 ORDER = (("x", "y", "z"), ("y", "z", "x"), ("z", "x", "y"))
-WAVES = (((2, 0, 384), (0, 384, 256), (1, 640, 384)), ((2, 1024, 384), (0, 1408, 384), (1, 1792, 256)))
+WAVES = (
+    ((2, 0, 256), (0, 256, 256), (1, 512, 256)),
+    ((2, 768, 512), (0, 1280, 384), (1, 1664, 384)),
+)
 PARTS = tuple(part for wave in WAVES for part in wave)
 FORTH = ((0, 1, 2), (3, 4, 5))
-BACK = ((3, 4, 5), (0, 1, 2))
+BACK = ((0, 1, 2), (3, 4, 5))
 
 
 def iota(shape, dim):
@@ -186,9 +189,16 @@
         copy.wait()
     weights = [pltpu.make_async_copy(wp_hbm, wp, w_sem.at[0])]
     weights[0].start()
-    attend_chunk(0)
+    early = 2
+
+    def attend_early(chunk, carry):
+        attend_chunk(chunk)
+        return carry
+
+    lax.fori_loop(0, early, attend_early, 0)
     pl.semaphore_wait(barrier, len(peers))
-    send_chunk(0)
+    for chunk in range(early):
+        send_chunk(chunk)
 
     for copy in inputs[8:]:
         copy.wait()
@@ -214,7 +224,7 @@
         send_chunk(chunk)
         return carry
 
-    lax.fori_loop(1, 4, attend_more, 0)
+    lax.fori_loop(early, 4, attend_more, 0)
     stat_t[...] = stat[...].T
     tops_a = Group(rec_stat.at[pl.ds(1, 7)])
     for k in (4, 3, 5, 2, 6, 1, 7):

time: 84.8 us -> 85.4 us (level)
  no operation moved by 1% of the time
where the time goes in v4:
time: 85.4 us; the launch traced here: 85.2 us
  Pallas kernels  83.7 us (98%)
  local copies, waits for them, and re-layouts  1.47 us (2%)
    pallas_call x1, Pallas kernels, shards(): pl.pallas_call(kernel, out_shape=jax.ShapeDtypeStruct((8, D), BF16), in_s...  83.7 us

profile of v4, /device:TPU:1, one launch (start us, length us, event | category | flops | bytes accessed | tf_op | source)
XLA Modules:
  0.0 85.2 jit_solution(2773915079807331091)
XLA Ops:
  0.0 83.7 %shard_map.154 = bf16[8,4096]{1,0:T(8,128)(2,1)} custom-call(bf16[64,32,128]{2,1,0:T(8,128)(2,1)} %q_hbm.1, bf16[64,2,128]{2,1,0:T(2,128)(2,1)} %nk_hbm.1, bf16[64,2,128]{2,1,0:T(2,128)(2,1)} %nv_hbm.1, bf16[64,2,32,128]{3,2,1,0:T(8,128)(2,1)} %kc_hbm.1, bf16[64,2,32,128]{3,2,1,0:T(8,128)(2,1)} %vc_hbm.1, s32[64]{0:T(128)} %len_hbm.1, ...), custom_call_target="tpu_custom_call" | custom-call | flops 10000000000 | bytes 27262976 | tf_op jit(solution)/shard_map/pallas_call | solution.py:521
  83.7 1.5 %copy.18 = bf16[8,4096]{1,0:T(8,128)(2,1)} copy(bf16[8,4096]{1,0:T(8,128)(2,1)} %shard_map.154) | data formatting | bytes 131072

commit v5 on v3

--- a/solution.py
+++ b/solution.py
@@ -17,10 +17,13 @@
 EPS = 1e-6
 LOW = -1e30
 ORDER = (("x", "y", "z"), ("y", "z", "x"), ("z", "x", "y"))
-WAVES = (((2, 0, 384), (0, 384, 256), (1, 640, 384)), ((2, 1024, 384), (0, 1408, 384), (1, 1792, 256)))
+WAVES = (
+    ((2, 0, 256), (0, 256, 256), (1, 512, 256)),
+    ((2, 768, 512), (0, 1280, 384), (1, 1664, 384)),
+)
 PARTS = tuple(part for wave in WAVES for part in wave)
 FORTH = ((0, 1, 2), (3, 4, 5))
-BACK = ((3, 4, 5), (0, 1, 2))
+BACK = ((0, 1, 2), (3, 4, 5))
 
 
 def iota(shape, dim):
@@ -37,7 +40,7 @@
     out_ref,
     q_ref, nk_ref, nv_ref, kc_ref, vc_ref, len_ref, res_ref, qg_ref, kg_ref, ng_ref, ids_ref, gw_ref,
     wp, wg, wu, wd,
-    num_f, num_b, stat, stat_t, coef, rec_num, rec_stat, attn,
+    q_n, q_s, num_f, num_b, stat, stat_t, coef, rec_num, rec_stat, attn,
     pair_s, pair_r, send_b, rec_b, hidden, sq_own, sq_rec,
     table_s, table_r, packed, meta, plane_meta, disp, comb,
     x_full, perm, perm_t, acc, act, act_p,
@@ -146,9 +149,8 @@
         bias = jnp.where(lane_pos < limit, 0.0, LOW)
         stats = jnp.zeros((8, 128), F32)
         for kv in range(2):
-            q = q_ref[rows, pl.ds(kv * 16, 16), :].astype(F32).reshape(128, 128)
-            q = q * lax.rsqrt(jnp.mean(q * q, axis=1, keepdims=True) + EPS) * qg_ref[...]
-            q = dot(shuffle, q.astype(BF16)).astype(BF16)
+            place = (lower // 8) * 2 + kv
+            q = q_s[:, place * 128 : place * 128 + 128]
             nk = nk_ref[rows, kv, :].astype(F32)
             nk = nk * lax.rsqrt(jnp.mean(nk * nk, axis=1, keepdims=True) + EPS) * kg_ref[...]
             nk = nk.astype(BF16).astype(F32)
@@ -178,6 +180,14 @@
         stat[rows, :] = stats
 
     def attend_chunk(chunk):
+        for sub in (0, 1):
+            rows = pl.ds(pl.multiple_of(chunk * 16 + sub * 8, 8), 8)
+            for kv in (0, 1):
+                q = q_ref[rows, pl.ds(kv * 16, 16), :].astype(F32).reshape(128, 128)
+                q = q * lax.rsqrt(jnp.mean(q * q, axis=1, keepdims=True) + EPS) * qg_ref[...]
+                place = sub * 2 + kv
+                q_n[:, place * 128 : place * 128 + 128] = q.astype(BF16)
+        q_s[...] = dot(shuffle, q_n[...]).astype(BF16)
         attend(chunk * 2, 0)
         attend(chunk * 2 + 1, 8)
         num_b[chunk] = num_f[...].astype(BF16)
@@ -519,7 +529,7 @@
             VMEM((8, D), BF16), VMEM((1, 128), F32), VMEM((1, 128), F32), VMEM((1, D), F32),
             VMEM((8, 8), jnp.int32), VMEM((8, 8), F32),
             VMEM((512, D), BF16), VMEM((D, FFW), BF16), VMEM((D, FFW), BF16), VMEM((FFW, D), BF16),
-            VMEM((32, 16, 128), F32), VMEM((4, 32, 16, 128), BF16), VMEM((128, 128), F32),
+            VMEM((128, 512), BF16), VMEM((128, 512), BF16), VMEM((32, 16, 128), F32), VMEM((4, 32, 16, 128), BF16), VMEM((128, 128), F32),
             VMEM((128, 128), F32), VMEM((128, 128), F32), VMEM((8, 4, 4, 16, 128), BF16),
             VMEM((8, 8, 128), F32), VMEM((64, 512), BF16),
             VMEM((2, 64, 1024), BF16), VMEM((2, 64, 1024), BF16), VMEM((2, 64, 1024), BF16),

time: 84.8 us -> 83.8 us (0.988)
  Pallas kernels: 83.2 us -> 82.1 us
    pallas_call x1, Pallas kernels: 83.2 us -> 82.1 us  [shards(): pl.pallas_call(kernel, out_shape=jax.ShapeDtypeStruct((8, D), BF16), in_s...]
where the time goes in v5:
time: 83.8 us; the launch traced here: 83.6 us
  Pallas kernels  82.1 us (98%)
  local copies, waits for them, and re-layouts  1.47 us (2%)
    pallas_call x1, Pallas kernels, shards(): pl.pallas_call(kernel, out_shape=jax.ShapeDtypeStruct((8, D), BF16), in_s...  82.1 us

profile of v5, /device:TPU:1, one launch (start us, length us, event | category | flops | bytes accessed | tf_op | source)
XLA Modules:
  0.0 83.6 jit_solution(13100660779288408944)
XLA Ops:
  0.0 82.1 %shard_map.154 = bf16[8,4096]{1,0:T(8,128)(2,1)} custom-call(bf16[64,32,128]{2,1,0:T(8,128)(2,1)} %q_hbm.1, bf16[64,2,128]{2,1,0:T(2,128)(2,1)} %nk_hbm.1, bf16[64,2,128]{2,1,0:T(2,128)(2,1)} %nv_hbm.1, bf16[64,2,32,128]{3,2,1,0:T(8,128)(2,1)} %kc_hbm.1, bf16[64,2,32,128]{3,2,1,0:T(8,128)(2,1)} %vc_hbm.1, s32[64]{0:T(128)} %len_hbm.1, ...), custom_call_target="tpu_custom_call" | custom-call | flops 10000000000 | bytes 27262976 | tf_op jit(solution)/shard_map/pallas_call | solution.py:521
  82.1 1.5 %copy.18 = bf16[8,4096]{1,0:T(8,128)(2,1)} copy(bf16[8,4096]{1,0:T(8,128)(2,1)} %shard_map.154) | data formatting | bytes 131072
